TPU v7x, 512 devices: a whole 4x8x8 slice. The times are simulated.
512 devices in a mesh: patch: 64 (over y, z), hist: 8 (over x, core).
Axes of the slice: x: 4, y: 8, z: 8, core: 2. Of those that a mesh axis runs over, the one named last changes fastest.
Arguments:
- zblocks: bfloat16 [8, 3072, 128, 128], P('hist', 'patch'), may hold values from -0.078125 to 0.078125
- slot_row: int32 [8, 3072], P('hist', 'patch'), may hold values from 0 to 7
- slot_offset: int32 [8, 3072], P('hist', 'patch'), may hold values from 0 to 8
- slot_delay: int32 [8, 3072], P('hist', 'patch'), may hold values from 0 to 1
- history: bfloat16 [16, 65536, 128], P('hist', 'patch'), may hold values from -6 to 6
- inverse: bfloat16 [65536, 128], P('patch'), may hold values from -0.5 to 0.5
- excite: bfloat16 [4, 65536, 128], P(None, 'patch'), may hold values from -6 to 6
Outputs:
- currents: bfloat16 [4, 65536, 128], P(None, ('patch', 'hist'))
All inputs are finite; a program needn't handle non-finite values.
Results may differ from a plain program's by a relative error of at most 0.0035.
Values may be sent and summed in bfloat16 or wider, within the bound.
A program may use at most 64 MiB of HBM per device.

v0:
```python
import jax
import jax.numpy as jnp
from jax import lax
from jax.sharding import PartitionSpec as P

R = 4
STEPS = 4


def extended(cells, sides, width):
    for axis, dim in sides:
        count = lax.axis_size(axis)
        ends = count - 1
        head = lax.slice_in_dim(cells, 0, width, axis=dim)
        tail = lax.slice_in_dim(cells, cells.shape[dim] - width, cells.shape[dim], axis=dim)
        cells = jnp.concatenate(
            [
                lax.ppermute(tail, axis, [(i, (i + 1) % count) for i in range(ends)]),
                cells,
                lax.ppermute(head, axis, [((i + 1) % count, i) for i in range(ends)]),
            ],
            axis=dim,
        )
    return cells


def shifted(block, axis, distance):
    devices = range(lax.axis_size(axis))
    route = [(i - distance, i) for i in devices if i - distance in devices]
    return lax.ppermute(block, axis, route)


def on_device(zblocks, slot_row, slot_offset, slot_delay, history, inverse, excite):
    blocksize = zblocks.shape[-1]
    unknowns = history.shape[1]
    columns = history.shape[2]
    nblocks = unknowns // blocksize
    nbands = lax.axis_size("hist")
    share_rows = unknowns // nbands
    band_index = lax.axis_index("hist")
    rim_rows = R * blocksize
    zmatrices = zblocks[0]
    row_ids = slot_row[0]
    col_ids = row_ids + slot_offset[0]
    delay_ids = slot_delay[0]
    select = (row_ids[None, :] == jnp.arange(nblocks, dtype=jnp.int32)[:, None]).astype(jnp.float32)
    results = []
    band_state = history
    for moment in range(STEPS):
        rimmed = extended(band_state, (("patch", 1),), rim_rows)
        blocked = rimmed.reshape(rimmed.shape[0], -1, blocksize, columns)
        picked = blocked[delay_ids, col_ids]
        products = jnp.einsum("sij,sjc->sic", zmatrices, picked, preferred_element_type=jnp.float32)
        summed = jnp.einsum("rs,sic->ric", select, products, precision=lax.Precision.HIGHEST)
        partial_value = summed.reshape(unknowns, columns)
        whole_sum = lax.psum(partial_value, "hist")
        residual = excite[moment].astype(jnp.float32) - whole_sum
        inv_blocks = inverse.astype(jnp.float32).reshape(-1, blocksize, blocksize)
        res_blocks = residual.reshape(-1, blocksize, columns)
        solved = jnp.einsum("bij,bjc->bic", inv_blocks, res_blocks, precision=lax.Precision.HIGHEST)
        current = solved.astype(jnp.bfloat16).reshape(-1, columns)
        own_rows = lax.dynamic_slice_in_dim(current, band_index * share_rows, share_rows, 0)
        results.append(own_rows)
        if moment + 1 < STEPS:
            oldest = shifted(band_state[-1], "hist", 1)
            incoming = jnp.where(band_index == 0, current, oldest)
            band_state = jnp.concatenate([incoming[None], band_state[:-1]], axis=0)
    return jnp.stack(results)


def solution(mesh):
    return jax.shard_map(
        on_device,
        mesh=mesh,
        in_specs=(
            P("hist", "patch", None, None),
            P("hist", "patch"),
            P("hist", "patch"),
            P("hist", "patch"),
            P("hist", "patch", None),
            P("patch", None),
            P(None, "patch", None),
        ),
        out_specs=P(None, ("patch", "hist"), None),
        check_vma=False,
    )
```

profile of v0, /device:TPU:40, one launch (start us, length us, event | category | flops | bytes accessed | tf_op | source)
XLA Modules:
  0.0 425.6 jit_solution(10601695170128031905)
XLA Ops:
  6.5 1.2 fusion.34
  7.7 4.3 %collective-permute-start = (bf16[2,512,128]{2,1,0:T(8,128)(2,1)S(1)}, bf16[2,512,128]{2,1,0:T(8,128)(2,1)S(1)}, u32[]{:S(2)}, u32[]{:S(2)}) collective-permute-start(bf16[2,512,128]{2,1,0:T(8,128)(2,1)S(1)} %get-tuple-element.11), channel_id=1, source_target_pairs={{0,8},{8,16},{16,24},{24,32},{32,40},{40,48},{48,56},{56,64},{64,7... | collective-permute-start | bytes 786440 | tf_op jit(solution)/shard_map/ppermute | solution.py:18
  12.0 9.4 %collective-permute-start.1 = (bf16[2,512,128]{2,1,0:T(8,128)(2,1)S(1)}, bf16[2,512,128]{2,1,0:T(8,128)(2,1)S(1)}, u32[]{:S(2)}, u32[]{:S(2)}) collective-permute-start(bf16[2,512,128]{2,1,0:T(8,128)(2,1)S(1)} %get-tuple-element.12), channel_id=1, source_target_pairs={{8,0},{16,8},{24,16},{32,24},{40,32},{48,40},{56,48},{64,56},{72,6... | collective-permute-start | bytes 786440 | tf_op jit(solution)/shard_map/ppermute | solution.py:20
  22.1 3.7 collective-permute-done
  25.8 1.2 collective-permute-done.1
  26.9 1.1 pad_maximum_fusion
  28.1 2.1 gather_fusion
  30.2 4.3 %fusion.14 = f32[48,128,128]{2,1,0:T(8,128)} fusion(bf16[48,128,128]{2,1,0:T(8,128)(2,1)} %gather_fusion, bf16[1,48,128,128]{3,2,1,0:T(8,128)(2,1)S(1)} %copy-done), kind=kOutput, calls=%fused_computation.18 | convolution fusion | flops 201326592 | bytes 6291456 | tf_op jit(solution)/shard_map/sij,sjc->sic/dot_general | solution.py:53
  34.5 3.6 copy.12
  38.0 3.1 fusion.6
  41.1 0.9 copy.8
  42.9 2.0 collective-permute-start.2
  44.9 67.7 %all-reduce.5.cloned.1.call-done = f32[1024,128]{1,0:T(8,128)} async-done(((f32[1024,128]{1,0:T(8,128)}), f32[1024,128]{1,0:T(8,128)}) %all-reduce.5.cloned.1.call-update) | async-done | bytes 524304 | tf_op jit(solution)/shard_map/psum | solution.py:56
  112.6 1.2 convert_subtract_fusion.3
  114.3 3.6 collective-permute-start.3
  117.8 5.1 %collective-permute-start.4 = (bf16[2,512,128]{2,1,0:T(8,128)(2,1)S(1)}, bf16[2,512,128]{2,1,0:T(8,128)(2,1)S(1)}, u32[]{:S(2)}, u32[]{:S(2)}) collective-permute-start(bf16[2,512,128]{2,1,0:T(8,128)(2,1)S(1)} %get-tuple-element.10), channel_id=1, source_target_pairs={{8,0},{16,8},{24,16},{32,24},{40,32},{48,40},{56,48},{64,56},{72,6... | collective-permute-start | bytes 786440 | tf_op jit(solution)/shard_map/ppermute | solution.py:20
  123.0 3.4 collective-permute-done.3
  126.3 1.2 collective-permute-done.4
  127.6 2.1 gather_fusion.1
  129.7 4.3 %fusion.12 = f32[48,128,128]{2,1,0:T(8,128)} fusion(bf16[48,128,128]{2,1,0:T(8,128)(2,1)} %gather_fusion.1, bf16[1,48,128,128]{3,2,1,0:T(8,128)(2,1)S(1)} %copy-done), kind=kOutput, calls=%fused_computation.16 | convolution fusion | flops 201326592 | bytes 6291456 | tf_op jit(solution)/shard_map/sij,sjc->sic/dot_general | solution.py:53
  134.0 3.6 copy.13
  137.5 3.1 fusion.4
  140.6 0.9 copy.9
  141.6 2.0 collective-permute-start.5
  143.6 70.5 %all-reduce.7.cloned.1.call-done = f32[1024,128]{1,0:T(8,128)} async-done(((f32[1024,128]{1,0:T(8,128)}), f32[1024,128]{1,0:T(8,128)}) %all-reduce.7.cloned.1.call-update) | async-done | bytes 524304 | tf_op jit(solution)/shard_map/psum | solution.py:56
  214.0 1.2 convert_subtract_fusion.2
  215.7 3.6 collective-permute-start.6
  219.3 5.1 %collective-permute-start.7 = (bf16[2,512,128]{2,1,0:T(8,128)(2,1)S(1)}, bf16[2,512,128]{2,1,0:T(8,128)(2,1)S(1)}, u32[]{:S(2)}, u32[]{:S(2)}) collective-permute-start(bf16[2,512,128]{2,1,0:T(8,128)(2,1)S(1)} %get-tuple-element.8), channel_id=1, source_target_pairs={{8,0},{16,8},{24,16},{32,24},{40,32},{48,40},{56,48},{64,56},{72,6... | collective-permute-start | bytes 786440 | tf_op jit(solution)/shard_map/ppermute | solution.py:20
  224.4 3.4 collective-permute-done.6
  227.7 1.2 collective-permute-done.7
  229.0 2.1 gather_fusion.2
  231.1 4.3 %fusion.10 = f32[48,128,128]{2,1,0:T(8,128)} fusion(bf16[48,128,128]{2,1,0:T(8,128)(2,1)} %gather_fusion.2, bf16[1,48,128,128]{3,2,1,0:T(8,128)(2,1)S(1)} %copy-done), kind=kOutput, calls=%fused_computation.14 | convolution fusion | flops 201326592 | bytes 6291456 | tf_op jit(solution)/shard_map/sij,sjc->sic/dot_general | solution.py:53
  235.4 3.6 copy.14
  238.9 3.0 fusion.2
  242.0 0.9 copy.10
  242.9 1.5 collective-permute-start.8
  244.4 71.0 %all-reduce.9.cloned.1.call-done = f32[1024,128]{1,0:T(8,128)} async-done(((f32[1024,128]{1,0:T(8,128)}), f32[1024,128]{1,0:T(8,128)}) %all-reduce.9.cloned.1.call-update) | async-done | bytes 524304 | tf_op jit(solution)/shard_map/psum | solution.py:56
  315.4 1.2 convert_subtract_fusion.1
  317.1 3.6 collective-permute-start.9
  320.6 5.1 %collective-permute-start.10 = (bf16[2,512,128]{2,1,0:T(8,128)(2,1)S(1)}, bf16[2,512,128]{2,1,0:T(8,128)(2,1)}, u32[]{:S(2)}, u32[]{:S(2)}) collective-permute-start(bf16[2,512,128]{2,1,0:T(8,128)(2,1)S(1)} %get-tuple-element.6), channel_id=1, source_target_pairs={{8,0},{16,8},{24,16},{32,24},{40,32},{48,40},{56,48},{64,56},{72,6... | collective-permute-start | bytes 786440 | tf_op jit(solution)/shard_map/ppermute | solution.py:20
  325.7 2.4 collective-permute-done.9
  329.6 1.1 pad_maximum_fusion.3
  330.7 2.1 gather_fusion.3
  332.8 4.3 %fusion.8 = f32[48,128,128]{2,1,0:T(8,128)} fusion(bf16[48,128,128]{2,1,0:T(8,128)(2,1)} %gather_fusion.3, bf16[1,48,128,128]{3,2,1,0:T(8,128)(2,1)S(1)} %copy-done), kind=kOutput, calls=%fused_computation.12 | convolution fusion | flops 201326592 | bytes 6291456 | tf_op jit(solution)/shard_map/sij,sjc->sic/dot_general | solution.py:53
  337.1 3.6 copy.15
  340.7 3.0 fusion
  346.9 69.9 %all-reduce.11.cloned.1.call-done = f32[1024,128]{1,0:T(8,128)} async-done(((f32[1024,128]{1,0:T(8,128)}), f32[1024,128]{1,0:T(8,128)}) %all-reduce.11.cloned.1.call-update) | async-done | bytes 524304 | tf_op jit(solution)/shard_map/psum | solution.py:56
  416.8 1.2 convert_subtract_fusion
  (50 shorter events, 9.1 us)
Async XLA Ops:
  6.5 23.6 %copy-start = (bf16[1,48,128,128]{3,2,1,0:T(8,128)(2,1)S(1)}, bf16[1,48,128,128]{3,2,1,0:T(8,128)(2,1)}, u32[]{:S(2)}) copy-start(bf16[1,48,128,128]{3,2,1,0:T(8,128)(2,1)} %param.7) | copy-start | bytes 4718596
  6.5 106.0 %all-reduce.5.cloned.1.call-start = ((), (), s32[]{:S(2)}) async-start(), calls=%async_computation | async-start | bytes 1048576 | tf_op jit(solution)/shard_map/psum | solution.py:56
  7.7 18.0 %collective-permute-start = (bf16[2,512,128]{2,1,0:T(8,128)(2,1)S(1)}, bf16[2,512,128]{2,1,0:T(8,128)(2,1)S(1)}, u32[]{:S(2)}, u32[]{:S(2)}) collective-permute-start(bf16[2,512,128]{2,1,0:T(8,128)(2,1)S(1)} %get-tuple-element.11), channel_id=1, source_target_pairs={{0,8},{8,16},{16,24},{24,32},{32,40},{40,48},{48,56},{56,64},{64,7... | collective-permute-start | bytes 786440 | tf_op jit(solution)/shard_map/ppermute | solution.py:18
  12.0 14.9 %collective-permute-start.1 = (bf16[2,512,128]{2,1,0:T(8,128)(2,1)S(1)}, bf16[2,512,128]{2,1,0:T(8,128)(2,1)S(1)}, u32[]{:S(2)}, u32[]{:S(2)}) collective-permute-start(bf16[2,512,128]{2,1,0:T(8,128)(2,1)S(1)} %get-tuple-element.12), channel_id=1, source_target_pairs={{8,0},{16,8},{24,16},{32,24},{40,32},{48,40},{56,48},{64,56},{72,6... | collective-permute-start | bytes 786440 | tf_op jit(solution)/shard_map/ppermute | solution.py:20
  34.5 3.6 copy-start.8
  38.0 4.1 copy-start.1
  41.1 72.6 %copy-start.2 = (bf16[1024,128]{1,0:T(8,128)(2,1)S(1)}, bf16[1024,128]{1,0:T(8,128)(2,1)}, u32[]{:S(2)}) copy-start(bf16[1024,128]{1,0:T(8,128)(2,1)} %param.12) | copy-start | bytes 786436
  42.0 172.0 %all-reduce.7.cloned.1.call-start = ((), (), s32[]{:S(2)}) async-start(), calls=%async_computation.1 | async-start | bytes 1048576 | tf_op jit(solution)/shard_map/psum | solution.py:56
  42.9 71.3 %collective-permute-start.2 = (bf16[1024,128]{1,0:T(8,128)(2,1)S(1)}, bf16[1024,128]{1,0:T(8,128)(2,1)}, u32[]{:S(2)}, u32[]{:S(2)}) collective-permute-start(bf16[1024,128]{1,0:T(8,128)(2,1)S(1)} %get-tuple-element.13), channel_id=1, source_target_pairs={{0,1},{1,2},{2,3},{3,4},{4,5},{5,6},{6,7},{8,9},{9,10},{10,11},{11... | collective-permute-start | bytes 786440 | tf_op jit(solution)/shard_map/ppermute | solution.py:30
  114.1 12.2 %copy-start.3 = (bf16[8,128,128]{1,2,0:T(8,128)(2,1)}, bf16[8,128,128]{1,2,0:T(8,128)(2,1)S(1)}, u32[]{:S(2)}) copy-start(bf16[8,128,128]{1,2,0:T(8,128)(2,1)S(1)} %convolution_convert_fusion.3) | copy-start | bytes 786436
  114.3 12.0 %collective-permute-start.3 = (bf16[2,512,128]{2,1,0:T(8,128)(2,1)S(1)}, bf16[2,512,128]{2,1,0:T(8,128)(2,1)S(1)}, u32[]{:S(2)}, u32[]{:S(2)}) collective-permute-start(bf16[2,512,128]{2,1,0:T(8,128)(2,1)S(1)} %get-tuple-element.9), channel_id=1, source_target_pairs={{0,8},{8,16},{16,24},{24,32},{32,40},{40,48},{48,56},{56,64},{64,7... | collective-permute-start | bytes 786440 | tf_op jit(solution)/shard_map/ppermute | solution.py:18
  117.8 9.6 %collective-permute-start.4 = (bf16[2,512,128]{2,1,0:T(8,128)(2,1)S(1)}, bf16[2,512,128]{2,1,0:T(8,128)(2,1)S(1)}, u32[]{:S(2)}, u32[]{:S(2)}) collective-permute-start(bf16[2,512,128]{2,1,0:T(8,128)(2,1)S(1)} %get-tuple-element.10), channel_id=1, source_target_pairs={{8,0},{16,8},{24,16},{32,24},{40,32},{48,40},{56,48},{64,56},{72,6... | collective-permute-start | bytes 786440 | tf_op jit(solution)/shard_map/ppermute | solution.py:20
  137.5 4.0 copy-start.6
  141.5 173.9 %all-reduce.9.cloned.1.call-start = ((), (), s32[]{:S(2)}) async-start(), calls=%async_computation.2 | async-start | bytes 1048576 | tf_op jit(solution)/shard_map/psum | solution.py:56
  141.6 74.0 %collective-permute-start.5 = (bf16[1024,128]{1,0:T(8,128)(2,1)S(1)}, bf16[1024,128]{1,0:T(8,128)(2,1)}, u32[]{:S(2)}, u32[]{:S(2)}) collective-permute-start(bf16[1024,128]{1,0:T(8,128)(2,1)S(1)} %copy-done.6), channel_id=1, source_target_pairs={{0,1},{1,2},{2,3},{3,4},{4,5},{5,6},{6,7},{8,9},{9,10},{10,11},{11... | collective-permute-start | bytes 786440 | tf_op jit(solution)/shard_map/ppermute | solution.py:30
  215.6 12.2 %copy-start.4 = (bf16[8,128,128]{1,2,0:T(8,128)(2,1)}, bf16[8,128,128]{1,2,0:T(8,128)(2,1)S(1)}, u32[]{:S(2)}) copy-start(bf16[8,128,128]{1,2,0:T(8,128)(2,1)S(1)} %convolution_convert_fusion.2) | copy-start | bytes 786436
  215.7 12.0 %collective-permute-start.6 = (bf16[2,512,128]{2,1,0:T(8,128)(2,1)S(1)}, bf16[2,512,128]{2,1,0:T(8,128)(2,1)S(1)}, u32[]{:S(2)}, u32[]{:S(2)}) collective-permute-start(bf16[2,512,128]{2,1,0:T(8,128)(2,1)S(1)} %get-tuple-element.7), channel_id=1, source_target_pairs={{0,8},{8,16},{16,24},{24,32},{32,40},{40,48},{48,56},{56,64},{64,7... | collective-permute-start | bytes 786440 | tf_op jit(solution)/shard_map/ppermute | solution.py:18
  219.3 9.6 %collective-permute-start.7 = (bf16[2,512,128]{2,1,0:T(8,128)(2,1)S(1)}, bf16[2,512,128]{2,1,0:T(8,128)(2,1)S(1)}, u32[]{:S(2)}, u32[]{:S(2)}) collective-permute-start(bf16[2,512,128]{2,1,0:T(8,128)(2,1)S(1)} %get-tuple-element.8), channel_id=1, source_target_pairs={{8,0},{16,8},{24,16},{32,24},{40,32},{48,40},{56,48},{64,56},{72,6... | collective-permute-start | bytes 786440 | tf_op jit(solution)/shard_map/ppermute | solution.py:20
  242.9 173.9 %all-reduce.11.cloned.1.call-start = ((), (), s32[]{:S(2)}) async-start(), calls=%async_computation.3 | async-start | bytes 1048576 | tf_op jit(solution)/shard_map/psum | solution.py:56
  242.9 74.0 %collective-permute-start.8 = (bf16[1024,128]{1,0:T(8,128)(2,1)S(1)}, bf16[1024,128]{1,0:T(8,128)(2,1)S(1)}, u32[]{:S(2)}, u32[]{:S(2)}) collective-permute-start(bf16[1024,128]{1,0:T(8,128)(2,1)S(1)} %broadcast_select_fusion), channel_id=1, source_target_pairs={{0,1},{1,2},{2,3},{3,4},{4,5},{5,6},{6,7},{8,9},{9,10},{10,11},{11... | collective-permute-start | bytes 786440 | tf_op jit(solution)/shard_map/ppermute | solution.py:30
  316.9 11.2 %copy-start.5 = (bf16[8,128,128]{1,2,0:T(8,128)(2,1)}, bf16[8,128,128]{1,2,0:T(8,128)(2,1)S(1)}, u32[]{:S(2)}) copy-start(bf16[8,128,128]{1,2,0:T(8,128)(2,1)S(1)} %convolution_convert_fusion.1) | copy-start | bytes 786436
  317.1 11.1 %collective-permute-start.9 = (bf16[2,512,128]{2,1,0:T(8,128)(2,1)S(1)}, bf16[2,512,128]{2,1,0:T(8,128)(2,1)S(1)}, u32[]{:S(2)}, u32[]{:S(2)}) collective-permute-start(bf16[2,512,128]{2,1,0:T(8,128)(2,1)S(1)} %get-tuple-element.5), channel_id=1, source_target_pairs={{0,8},{8,16},{16,24},{24,32},{32,40},{40,48},{48,56},{56,64},{64,7... | collective-permute-start | bytes 786440 | tf_op jit(solution)/shard_map/ppermute | solution.py:18
  320.6 9.0 %collective-permute-start.10 = (bf16[2,512,128]{2,1,0:T(8,128)(2,1)S(1)}, bf16[2,512,128]{2,1,0:T(8,128)(2,1)}, u32[]{:S(2)}, u32[]{:S(2)}) collective-permute-start(bf16[2,512,128]{2,1,0:T(8,128)(2,1)S(1)} %get-tuple-element.6), channel_id=1, source_target_pairs={{8,0},{16,8},{24,16},{32,24},{40,32},{48,40},{56,48},{64,56},{72,6... | collective-permute-start | bytes 786440 | tf_op jit(solution)/shard_map/ppermute | solution.py:20
  328.1 0.7 copy-start.7
Sparse Core Ops, SparseCore 0:
  42.2 70.3 all-reduce.4
  141.6 72.3 all-reduce.6
  243.0 72.3 all-reduce.8
  344.7 72.0 all-reduce.10
where the time goes:
time: 427 us; the launch traced here: 426 us
  waiting for transfers between devices  296 us (69%)
  starting transfers between devices  45.2 us (11%)
  local copies, waits for them, and re-layouts  31.3 us (7%)
  matrix products  30.9 us (7%)
  between operations  13.4 us (3%)
  other arithmetic  8.61 us (2%)
    psum x4, waiting for transfers between devices, on_device(): whole_sum = lax.psum(partial_value, 'hist')  279 us
    ppermute x4, starting transfers between devices, extended(): lax.ppermute(head, axis, [((i + 1) % count, i) for i in range(ends)])  24.7 us
    dot_general x4, matrix products, on_device(): jnp.einsum('sij,sjc->sic', zmatrices, picked, preferred_element_type=jnp....  17.1 us
    ppermute x4, starting transfers between devices, extended(): lax.ppermute(tail, axis, [(i, (i + 1) % count) for i in range(ends)])  14.9 us
    dot_general x4, local copies, waits for them, and re-layouts, on_device(): jnp.einsum('sij,sjc->sic', zmatrices, picked, preferred_element_type=jnp....  14.2 us
    ppermute x4, waiting for transfers between devices, extended(): lax.ppermute(tail, axis, [(i, (i + 1) % count) for i in range(ends)])  12.8 us
    dot_general x4, matrix products, on_device(): jnp.einsum('rs,sic->ric', select, products, precision=lax.Precision.HIGHEST)  12.2 us
  transfers between devices with their start and end apart: 15, of which 12 were waited for; matrix products, arithmetic and copies ran while one was open for 2% of the time, Pallas kernels for 0%

commit v1 on v0

v1 whole, which is shorter than its diff:
```python
import jax
import jax.numpy as jnp
from jax import lax
from jax.experimental import pallas as pl
from jax.experimental.pallas import tpu as pltpu
from jax.sharding import PartitionSpec as P

R = 4
STEPS = 4
ROWS = 8
HALF = ROWS // 2
GROUP = 8
BF16 = jnp.bfloat16
F32 = jnp.float32


def kernel(
    z_hbm, row_ref, off_ref, dly_ref, hist_hbm, inv_hbm, exc_hbm, out_hbm,
    xb0, xb1, xb2, xb3, xb4, xb5, zbuf, sums, stage, twin, mixed, tree, far, near, excv, invv,
    col_s, prev_s, last_s,
    load_sem, halo_send, halo_recv, shift_send, shift_recv,
    twin_send, twin_recv, red_send, red_recv, tree_recv, out_send, out_recv, near_recv,
):
    xb = (xb0, xb1, xb2, xb3, xb4, xb5)
    cap, bs, _ = z_hbm.shape
    p = lax.axis_index("patch")
    h = lax.axis_index("hist")
    p_last = lax.axis_size("patch") - 1
    h_last = lax.axis_size("hist") - 1
    odd = h % 2
    has_left = p > 0
    has_right = p < p_last

    def patch(q):
        return {"patch": q}

    def band(q):
        return {"hist": q}

    def load(i):
        pairs = (
            (hist_hbm.at[1], xb0.at[pl.ds(R, ROWS)]),
            (hist_hbm.at[0], xb1.at[pl.ds(R, ROWS)]),
            (z_hbm, zbuf),
            (inv_hbm, invv),
            (exc_hbm, excv),
        )
        return pltpu.make_async_copy(pairs[i][0], pairs[i][1], load_sem.at[i])

    for i in range(3):
        load(i).start()

    @pl.when(h == 0)
    def _():
        load(3).start()
        load(4).start()

    barrier = pltpu.get_barrier_semaphore()

    def greet(where):
        pl.semaphore_signal(barrier, inc=1, device_id=where, device_id_type=pl.DeviceIdType.MESH)

    @pl.when(has_left)
    def _():
        greet(patch(p - 1))

    @pl.when(has_right)
    def _():
        greet(patch(p + 1))

    @pl.when(h == 0)
    def _():
        for q in range(1, GROUP):
            greet(band(q))

    @pl.when(h > 0)
    def _():
        greet(band(0))

    @pl.when(h > 1)
    def _():
        greet(band(h - 1))

    @pl.when((h > 0) & (h < h_last))
    def _():
        greet(band(h + 1))

    for a, b in ((2, 4), (4, 2), (5, 7), (7, 5)):
        @pl.when(h == a)
        def _(b=b):
            greet(band(b))

    pairs = jnp.where(h == 0, GROUP - 1, 1)
    pairs = pairs + jnp.where(h > 1, 1, 0) + jnp.where((h > 0) & (h < h_last), 1, 0)
    pairs = pairs + jnp.where((h == 2) | (h == 4) | (h == 5) | (h == 7), 1, 0)
    pairs = pairs + jnp.where(has_left, 1, 0) + jnp.where(has_right, 1, 0)
    pl.semaphore_wait(barrier, pairs)

    def remote(src, dst, ssem, rsem, where):
        return pltpu.make_async_remote_copy(
            src_ref=src, dst_ref=dst, send_sem=ssem, recv_sem=rsem,
            device_id=where, device_id_type=pl.DeviceIdType.MESH,
        )

    def to_left(j):
        src = hist_hbm.at[1 - j, pl.ds(0, R)] if j < 2 else xb[j].at[pl.ds(R, R)]
        return remote(src, xb[j].at[pl.ds(R + ROWS, R)], halo_send.at[j, 0], halo_recv.at[j, 1], patch(p - 1))

    def to_right(j):
        src = hist_hbm.at[1 - j, pl.ds(ROWS - R, R)] if j < 2 else xb[j].at[pl.ds(ROWS, R)]
        return remote(src, xb[j].at[pl.ds(0, R)], halo_send.at[j, 1], halo_recv.at[j, 0], patch(p + 1))

    def halo_start(j):
        @pl.when(has_left)
        def _():
            to_left(j).start()

        @pl.when(has_right)
        def _():
            to_right(j).start()

    def halo_wait(j):
        @pl.when(has_left)
        def _():
            to_right(j).wait_recv()

        @pl.when(has_right)
        def _():
            to_left(j).wait_recv()

    def halo_sent(j):
        @pl.when(has_left)
        def _():
            to_left(j).wait_send()

        @pl.when(has_right)
        def _():
            to_right(j).wait_send()

    def shift(j):
        src = hist_hbm.at[1 - j] if j < 2 else xb[j].at[pl.ds(R, ROWS)]
        return remote(src, xb[j + 2].at[pl.ds(R, ROWS)], shift_send.at[j], shift_recv.at[j], band(h + 1))

    def shift_start(j):
        @pl.when(h < h_last)
        def _():
            shift(j).start()

    halo_start(0)
    halo_start(1)
    shift_start(0)
    shift_start(1)

    @pl.when(p == 0)
    def _():
        for j in range(5):
            xb[j][pl.ds(0, R)] = jnp.zeros((R,) + xb[j].shape[1:], BF16)

    @pl.when(p == p_last)
    def _():
        for j in range(5):
            xb[j][pl.ds(R + ROWS, R)] = jnp.zeros((R,) + xb[j].shape[1:], BF16)

    sums[cap] = jnp.zeros(sums.shape[1:], F32)

    def note(s, last):
        row = row_ref[0, s]
        col_s[s] = row + off_ref[0, s]
        before = jnp.int32(cap)
        for r in range(ROWS):
            before = jnp.where(row == r, last[r], before)
        prev_s[s] = before
        return tuple(jnp.where(row == r, s, last[r]) for r in range(ROWS))

    last = lax.fori_loop(0, cap, note, (jnp.int32(cap),) * ROWS)
    for r in range(ROWS):
        last_s[r] = last[r]

    def products(n):
        width = 8 if cap % 8 == 0 else 1

        def some(t, carry):
            for i in range(width):
                s = t * width + i
                col = col_s[s]
                late = dly_ref[0, s]
                x = jnp.where(late == 1, xb[n][col], xb[n + 1][col])
                sums[s] = sums[prev_s[s]] + jnp.dot(zbuf[s], x, preferred_element_type=F32)
            return carry

        lax.fori_loop(0, cap // width, some, 0)

    def row_sum(r):
        return sums[last_s[r]]

    def twin_copy(n):
        return remote(
            stage.at[n, pl.ds(HALF * (1 - odd), HALF)], twin.at[n], twin_send.at[n], twin_recv.at[n],
            band(h + 1 - 2 * odd),
        )

    def near_copy(n):
        return remote(stage.at[n], near.at[n], twin_send.at[n], near_recv.at[n], band(0))

    def far_copy(n, k):
        return remote(mixed.at[n], far.at[n, k], red_send.at[n], red_recv.at[n, k], band(0))

    def tree_copy(n, q):
        return remote(mixed.at[n], tree.at[n], red_send.at[n], tree_recv.at[n], band(q))

    far_from = ((2, 0), (3, 1), (6, 2), (7, 3))

    def out_copy(n, r):
        return remote(xb[n + 2].at[R + r], out_hbm.at[n], out_send.at[n, r], out_recv.at[n], band(r))

    def own_copy(n):
        return pltpu.make_async_copy(xb[n + 2].at[R], out_hbm.at[n], out_send.at[n, 0])

    def solve(n):
        near_copy(n).wait_recv()
        for k in range(4):
            far_copy(n, k).wait_recv()
        for r in range(ROWS):
            total = row_sum(r) + near[n, r]
            for k in ((0, 2) if r < HALF else (1, 3)):
                total = total + far[n, k, r % HALF].astype(F32)
            residual = excv[n, r].astype(F32) - total
            high = residual.astype(BF16)
            low = (residual - high.astype(F32)).astype(BF16)
            inverse = invv[r]
            current = jnp.dot(inverse, high, preferred_element_type=F32) + jnp.dot(
                inverse, low, preferred_element_type=F32
            )
            xb[n + 2][R + r] = current.astype(BF16)
            if n < 3 and r == HALF - 1:
                @pl.when(has_left)
                def _():
                    to_left(n + 2).start()
            if n < 3 and r == ROWS - 1:
                @pl.when(has_right)
                def _():
                    to_right(n + 2).start()
        if n == 0:
            shift(2).start()
        own_copy(n).start()
        for r in range(1, ROWS):
            out_copy(n, r).start()

    def share(n):
        for r in range(ROWS):
            stage[n, r] = row_sum(r)

        @pl.when(h == 1)
        def _():
            near_copy(n).start()

        @pl.when(h > 1)
        def _():
            twin_copy(n).start()

    def merge(n):
        @pl.when(h > 1)
        def _():
            twin_copy(n).wait_recv()

            @pl.when((h == 2) | (h == 7))
            def _():
                tree_copy(n, 0).wait_recv()
                for i in range(HALF):
                    mixed[n, i] = (stage[n, HALF * odd + i] + twin[n, i] + tree[n, i].astype(F32)).astype(BF16)

            @pl.when((h != 2) & (h != 7))
            def _():
                for i in range(HALF):
                    mixed[n, i] = (stage[n, HALF * odd + i] + twin[n, i]).astype(BF16)

            for a, b in ((4, 2), (5, 7)):
                @pl.when(h == a)
                def _(b=b):
                    tree_copy(n, b).start()

            for a, k in far_from:
                @pl.when(h == a)
                def _(k=k):
                    far_copy(n, k).start()

    for i in range(3):
        load(i).wait()

    @pl.when(h == 0)
    def _():
        load(3).wait()
        load(4).wait()

    halo_wait(0)
    halo_wait(1)

    @pl.when(h > 0)
    def _():
        shift(0).wait_recv()
        halo_start(2)
        shift_start(2)

    for n in range(STEPS):
        if n > 0:
            halo_wait(n + 1)
        products(n)

        @pl.when(h == 0)
        def _(n=n):
            solve(n)

        @pl.when(h > 0)
        def _(n=n):
            share(n)
            if n == 0:
                shift(1).wait_recv()
                halo_start(3)
            merge(n)
            if n == 0:
                @pl.when(h > 1)
                def _():
                    shift(2).wait_recv()
                    halo_start(4)
            if n == 2:
                @pl.when(h == 1)
                def _():
                    shift(2).wait_recv()
                    halo_start(4)

    @pl.when(h == 0)
    def _():
        for n in range(STEPS):
            own_copy(n).wait()
            for r in range(1, ROWS):
                out_copy(n, r).wait_send()

    @pl.when(h == 1)
    def _():
        for n in range(STEPS):
            near_copy(n).wait_send()

    @pl.when(h > 1)
    def _():
        for n in range(STEPS):
            twin_copy(n).wait_send()
            far_copy(n, 0).wait_send()

    for j in range(5):
        halo_sent(j)

    @pl.when(h < h_last)
    def _():
        for j in range(3):
            shift(j).wait_send()

    @pl.when(h > 0)
    def _():
        for n in range(STEPS):
            out_copy(n, 0).wait_recv()


def on_device(zblocks, slot_row, slot_offset, slot_delay, history, inverse, excite):
    _, cap, bs, _ = zblocks.shape
    columns = history.shape[2]
    slots = zblocks[0]
    past = history.reshape(history.shape[0], ROWS, bs, columns)
    inv = inverse.reshape(ROWS, bs, bs)
    exc = excite.reshape(STEPS, ROWS, bs, columns)
    any_spec = pl.BlockSpec(memory_space=pl.ANY)
    smem_spec = pl.BlockSpec(memory_space=pltpu.SMEM)
    block = (bs, columns)
    dma = pltpu.SemaphoreType.DMA
    return pl.pallas_call(
        kernel,
        out_shape=jax.ShapeDtypeStruct((STEPS, bs, columns), BF16),
        in_specs=[any_spec, smem_spec, smem_spec, smem_spec, any_spec, any_spec, any_spec],
        out_specs=any_spec,
        scratch_shapes=[pltpu.VMEM((ROWS + 2 * R,) + block, BF16) for _ in range(6)]
        + [
            pltpu.VMEM((cap, bs, bs), BF16),
            pltpu.VMEM((cap + 1,) + block, F32),
            pltpu.VMEM((STEPS, ROWS) + block, F32),
            pltpu.VMEM((STEPS, HALF) + block, F32),
            pltpu.VMEM((STEPS, HALF) + block, BF16),
            pltpu.VMEM((STEPS, HALF) + block, BF16),
            pltpu.VMEM((STEPS, 4, HALF) + block, BF16),
            pltpu.VMEM((STEPS, ROWS) + block, F32),
            pltpu.VMEM((STEPS, ROWS) + block, BF16),
            pltpu.VMEM((ROWS, bs, bs), BF16),
            pltpu.SMEM((cap,), jnp.int32),
            pltpu.SMEM((cap,), jnp.int32),
            pltpu.SMEM((ROWS,), jnp.int32),
            dma((5,)),
            dma((5, 2)),
            dma((5, 2)),
            dma((3,)),
            dma((3,)),
            dma((STEPS,)),
            dma((STEPS,)),
            dma((STEPS,)),
            dma((STEPS, 4)),
            dma((STEPS,)),
            dma((STEPS, ROWS)),
            dma((STEPS,)),
            dma((STEPS,)),
        ],
        compiler_params=pltpu.CompilerParams(
            collective_id=0, has_side_effects=True, vmem_limit_bytes=40 * 1024 * 1024
        ),
    )(slots, slot_row, slot_offset, slot_delay, past, inv, exc)


def solution(mesh):
    return jax.shard_map(
        on_device,
        mesh=mesh,
        in_specs=(
            P("hist", "patch", None, None),
            P("hist", "patch"),
            P("hist", "patch"),
            P("hist", "patch"),
            P("hist", "patch", None),
            P("patch", None),
            P(None, "patch", None),
        ),
        out_specs=P(None, ("patch", "hist"), None),
        check_vma=False,
    )
```

time: 427 us -> 65.9 us (0.15)
  the two profiles are of different devices: /device:TPU:40 before, /device:TPU:37 now
where the time goes in v1:
time: 65.9 us; the launch traced here: 65.6 us
  Pallas kernels  58.3 us (88%)
  local copies, waits for them, and re-layouts  7.24 us (11%)
    pallas_call x1, Pallas kernels, on_device(): pl.pallas_call(kernel, out_shape=jax.ShapeDtypeStruct((STEPS, bs, columns...  58.3 us
    unnamed x15, local copies, waits for them, and re-layouts  7.24 us

profile of v1, /device:TPU:37, one launch (start us, length us, event | category | flops | bytes accessed | tf_op | source)
XLA Modules:
  0.0 65.6 jit_solution(13997460314324938306)
XLA Ops:
  0.0 0.0 copy-start
  0.0 1.4 %copy-done = bf16[1,48,128,128]{3,2,1,0:T(8,128)(2,1)S(1)} copy-done((bf16[1,48,128,128]{3,2,1,0:T(8,128)(2,1)S(1)}, bf16[1,48,128,128]{3,2,1,0:T(8,128)(2,1)}, u32[]{:S(2)}) %copy-start) | copy-done | bytes 1572888
  1.4 0.0 copy-start.1
  1.4 1.2 %copy-done.1 = bf16[4,1024,128]{2,1,0:T(8,128)(2,1)S(1)} copy-done((bf16[4,1024,128]{2,1,0:T(8,128)(2,1)S(1)}, bf16[4,1024,128]{2,1,0:T(8,128)(2,1)}, u32[]{:S(2)}) %copy-start.1) | copy-done | bytes 1048600
  2.6 0.0 copy-start.2
  2.6 1.0 %copy-done.2 = bf16[2,1024,128]{2,1,0:T(8,128)(2,1)S(1)} copy-done((bf16[2,1024,128]{2,1,0:T(8,128)(2,1)S(1)}, bf16[2,1024,128]{2,1,0:T(8,128)(2,1)}, u32[]{:S(2)}) %copy-start.2) | copy-done | bytes 524312
  3.7 0.0 copy-start.3
  3.7 0.9 %copy-done.3 = bf16[1024,128]{1,0:T(8,128)(2,1)S(1)} copy-done((bf16[1024,128]{1,0:T(8,128)(2,1)S(1)}, bf16[1024,128]{1,0:T(8,128)(2,1)}, u32[]{:S(2)}) %copy-start.3) | copy-done | bytes 262168
  4.6 0.0 copy-start.4
  4.6 0.7 copy-done.4
  5.3 0.0 copy-start.5
  5.3 0.7 copy-done.5
  5.9 0.0 copy-start.6
  5.9 0.7 copy-done.6
  6.6 58.3 %shard_map.73 = bf16[4,128,128]{2,1,0:T(8,128)(2,1)S(1)} custom-call(bf16[48,128,128]{2,1,0:T(8,128)(2,1)S(1)} %bitcast.4, s32[1,48]{1,0:T(1,128)S(1)} %copy-done.4, s32[1,48]{1,0:T(1,128)S(1)} %copy-done.5, s32[1,48]{1,0:T(1,128)S(1)} %copy-done.6, bf16[2,8,128,128]{3,2,1,0:T(8,128)(2,1)S(1)} %bitcast.6, bf16[8,128,128]{2,1,0:T(8,128)(2,1)S(1)} %bitcast.7, ...), custom_call_target="tpu_custom_call" | custom-call | tf_op jit(solution)/shard_map/pallas_call | solution.py:374
  64.9 0.7 %copy.9 = bf16[4,128,128]{2,1,0:T(8,128)(2,1)} copy(bf16[4,128,128]{2,1,0:T(8,128)(2,1)S(1)} %shard_map.73) | data formatting | bytes 262144
Async XLA Ops:
  0.0 1.4 %copy-start = (bf16[1,48,128,128]{3,2,1,0:T(8,128)(2,1)S(1)}, bf16[1,48,128,128]{3,2,1,0:T(8,128)(2,1)}, u32[]{:S(2)}) copy-start(bf16[1,48,128,128]{3,2,1,0:T(8,128)(2,1)} %param.7) | copy-start | bytes 4718596
  1.4 1.2 %copy-start.1 = (bf16[4,1024,128]{2,1,0:T(8,128)(2,1)S(1)}, bf16[4,1024,128]{2,1,0:T(8,128)(2,1)}, u32[]{:S(2)}) copy-start(bf16[4,1024,128]{2,1,0:T(8,128)(2,1)} %param.13) | copy-start | bytes 3145732
  2.6 1.0 %copy-start.2 = (bf16[2,1024,128]{2,1,0:T(8,128)(2,1)S(1)}, bf16[2,1024,128]{2,1,0:T(8,128)(2,1)}, u32[]{:S(2)}) copy-start(bf16[2,1024,128]{2,1,0:T(8,128)(2,1)} %param.11) | copy-start | bytes 1572868
  3.7 0.9 %copy-start.3 = (bf16[1024,128]{1,0:T(8,128)(2,1)S(1)}, bf16[1024,128]{1,0:T(8,128)(2,1)}, u32[]{:S(2)}) copy-start(bf16[1024,128]{1,0:T(8,128)(2,1)} %param.12) | copy-start | bytes 786436
  4.6 0.7 copy-start.4
  5.3 0.7 copy-start.5
  5.9 0.7 copy-start.6

commit v2 on v1

v2 whole, which is shorter than its diff:
```python
import jax
import jax.numpy as jnp
from jax import lax
from jax.experimental import pallas as pl
from jax.experimental.pallas import tpu as pltpu
from jax.sharding import PartitionSpec as P

R = 4
STEPS = 4
ROWS = 8
HALF = ROWS // 2
GROUP = 8
MARCH = 1
BF16 = jnp.bfloat16
F32 = jnp.float32
ORDER = (0, 4, 1, 5, 2, 6, 3, 7)


def kernel(
    z_hbm, row_hbm, off_hbm, dly_hbm, hist_hbm, inv_hbm, exc_hbm, out_hbm,
    xb0, xb1, xb2, xb3, xb4, xb5, zbuf, sums, stage, twin, mixed, tree, far, excv, invv,
    row_s, off_s, dly_s, col_s, prev_s, last_s,
    load_sem, swap_send, halo_send, halo_recv, shift_send, shift_recv,
    twin_send, twin_recv, red_send, far_recv, tree_recv, out_send, out_recv,
):
    xb = (xb0, xb1, xb2, xb3, xb4, xb5)
    cap = z_hbm.shape[0]
    p = lax.axis_index("patch")
    h = lax.axis_index("hist")
    p_last = lax.axis_size("patch") - 1
    h_last = lax.axis_size("hist") - 1
    odd = h % 2
    first = h < 2
    has_left = p > 0
    has_right = p < p_last

    def when(condition):
        return pl.when(condition)

    def at(patch=p, hist=h):
        return {"patch": patch, "hist": hist}

    barrier = pltpu.get_barrier_semaphore()

    def greet(where):
        pl.semaphore_signal(barrier, inc=1, device_id=where, device_id_type=pl.DeviceIdType.MESH)

    def when_greet(condition, where):
        @when(condition)
        def _():
            greet(where)

    when_greet(has_left, at(patch=p - 1))
    when_greet(has_right, at(patch=p + 1))
    when_greet(has_left & first, at(patch=p - 1, hist=1 - h))
    when_greet(has_right & first, at(patch=p + 1, hist=1 - h))
    lines = ((1, 2), (0, 2, 3, 4, 5, 6, 7), (0, 1, 3), (1, 2, 4, 5), (1, 3, 5), (1, 3, 4, 6, 7), (1, 5, 7), (1, 5, 6))
    met = jnp.int32(0)
    for a, others in enumerate(lines):
        @when(h == a)
        def _(others=others):
            for b in others:
                greet(at(hist=b))

        met = jnp.where(h == a, len(others), met)
    sides = jnp.where(has_left, 1, 0) + jnp.where(has_right, 1, 0)
    met = met + sides * jnp.where(first, 2, 1)

    def remote(src, dst, ssem, rsem, where):
        return pltpu.make_async_remote_copy(
            src_ref=src, dst_ref=dst, send_sem=ssem, recv_sem=rsem,
            device_id=where, device_id_type=pl.DeviceIdType.MESH,
        )

    tables = ((row_hbm, row_s), (off_hbm, off_s), (dly_hbm, dly_s))
    loads = tables + (
        (hist_hbm.at[1], xb0.at[pl.ds(R, ROWS)]),
        (hist_hbm.at[0], xb1.at[pl.ds(R, ROWS)]),
        (z_hbm, zbuf),
    )
    march_loads = ((inv_hbm, invv), (exc_hbm, excv))

    def load(i):
        return pltpu.make_async_copy(loads[i][0], loads[i][1], load_sem.at[i])

    def swap(i):
        return remote(loads[i][0], loads[i][1], swap_send.at[i], load_sem.at[i], at(hist=1 - h))

    def march_load(i):
        return pltpu.make_async_copy(march_loads[i][0], march_loads[i][1], load_sem.at[len(loads) + i])

    def load_wait(i):
        @when(first)
        def _():
            swap(i).wait_recv()

        @when(jnp.logical_not(first))
        def _():
            load(i).wait()

    low, high = pl.ds(0, R), pl.ds(R + ROWS, R)

    def to_left(j, q=None):
        if j < 2:
            src = hist_hbm.at[1 - j, pl.ds(0, R)]
            hist = jnp.where(first, 1 - h, h)
        else:
            src = xb[j].at[pl.ds(R, R)]
            hist = h
        dst = xb[j].at[high]
        if q is not None:
            src, dst = xb[j].at[R + q], xb[j].at[R + ROWS + q]
        return remote(src, dst, halo_send.at[j, 0], halo_recv.at[j, 1], at(patch=p - 1, hist=hist))

    def to_right(j, q=None):
        if j < 2:
            src = hist_hbm.at[1 - j, pl.ds(ROWS - R, R)]
            hist = jnp.where(first, 1 - h, h)
        else:
            src = xb[j].at[pl.ds(ROWS, R)]
            hist = h
        dst = xb[j].at[low]
        if q is not None:
            src, dst = xb[j].at[ROWS + q], xb[j].at[q]
        return remote(src, dst, halo_send.at[j, 1], halo_recv.at[j, 0], at(patch=p + 1, hist=hist))

    def halo_start(j):
        @when(has_left)
        def _():
            to_left(j).start()

        @when(has_right)
        def _():
            to_right(j).start()

    def halo_wait(j):
        @when(has_left)
        def _():
            to_right(j).wait_recv()

        @when(has_right)
        def _():
            to_left(j).wait_recv()

    def halo_sent(j):
        @when(has_left)
        def _():
            to_left(j).wait_send()

        @when(has_right)
        def _():
            to_right(j).wait_send()

    def shift(j):
        src = hist_hbm.at[1 - j] if j < 2 else xb[2].at[pl.ds(R, ROWS)]
        to = h + 1 if j < 2 else jnp.where(h == 1, 0, jnp.where(h == 0, 2, h + 1))
        return remote(src, xb[j + 2].at[pl.ds(R, ROWS)], shift_send.at[j], shift_recv.at[j], at(hist=to))

    def shift_here(j):
        return pltpu.make_async_copy(hist_hbm.at[1 - j], xb[j + 2].at[pl.ds(R, ROWS)], shift_recv.at[j])

    def shift_start(j):
        @when(h == 0)
        def _():
            shift_here(j).start()

        @when((h > 0) & (h < h_last))
        def _():
            shift(j).start()

    def shift_wait(j):
        @when(h == 0)
        def _():
            shift_here(j).wait()

        @when(h > 1)
        def _():
            shift(j).wait_recv()

    @when(jnp.logical_not(first))
    def _():
        for i in range(len(loads)):
            load(i).start()

    @when(h == MARCH)
    def _():
        for i in range(2):
            march_load(i).start()

    pl.semaphore_wait(barrier, met)
    halo_start(0)
    halo_start(1)

    @when(first)
    def _():
        for i in range(len(loads)):
            swap(i).start()

    shift_start(0)
    shift_start(1)

    @when(p == 0)
    def _():
        for j in range(5):
            xb[j][low] = jnp.zeros((R,) + xb[j].shape[1:], BF16)

    @when(p == p_last)
    def _():
        for j in range(5):
            xb[j][high] = jnp.zeros((R,) + xb[j].shape[1:], BF16)

    sums[cap] = jnp.zeros(sums.shape[1:], F32)
    for i in range(3):
        load_wait(i)

    def note(s, last):
        row = row_s[0, s]
        col_s[s] = row + off_s[0, s]
        before = jnp.int32(cap)
        for r in range(ROWS):
            before = jnp.where(row == r, last[r], before)
        prev_s[s] = before
        return tuple(jnp.where(row == r, s, last[r]) for r in range(ROWS))

    last = lax.fori_loop(0, cap, note, (jnp.int32(cap),) * ROWS)
    for r in range(ROWS):
        last_s[r] = last[r]

    def products(n):
        for s in range(cap):
            col = col_s[s]
            x = jnp.where(dly_s[0, s] == 1, xb[n][col], xb[n + 1][col])
            sums[s] = sums[prev_s[s]] + jnp.dot(zbuf[s], x, preferred_element_type=F32)

    def row_sum(r):
        return sums[last_s[r]]

    def twin_copy(n):
        return remote(stage.at[n], twin.at[n], twin_send.at[n], twin_recv.at[n], at(hist=h + 1))

    def far_copy(n, k, r):
        return remote(mixed.at[n, r], far.at[n, k, r], red_send.at[n, r], far_recv.at[n, k, r], at(hist=MARCH))

    def tree_copy(n, r):
        to = 3 if r < HALF else 7
        return remote(mixed.at[n, r], tree.at[n, r % HALF], red_send.at[n, r], tree_recv.at[n, r % HALF], at(hist=to))

    def out_copy(n, r):
        return remote(xb[n + 2].at[R + r], out_hbm.at[n], out_send.at[n, r], out_recv.at[n], at(hist=r))

    def own_copy(n):
        return pltpu.make_async_copy(xb[n + 2].at[R + MARCH], out_hbm.at[n], out_send.at[n, MARCH])

    def solve(n):
        twin_copy(n).wait_recv()
        for r in ORDER:
            for k in range(2):
                far_copy(n, k, r).wait_recv()
            total = row_sum(r) + twin[n, r].astype(F32) + far[n, 0, r].astype(F32) + far[n, 1, r].astype(F32)
            residual = excv[n, r].astype(F32) - total
            coarse = residual.astype(BF16)
            fine = (residual - coarse.astype(F32)).astype(BF16)
            inverse = invv[r]
            current = jnp.dot(inverse, coarse, preferred_element_type=F32) + jnp.dot(
                inverse, fine, preferred_element_type=F32
            )
            xb[n + 2][R + r] = current.astype(BF16)
            if n < STEPS - 1:
                if r < HALF:
                    @when(has_left)
                    def _(r=r):
                        to_left(n + 2, r).start()
                else:
                    @when(has_right)
                    def _(r=r):
                        to_right(n + 2, r - HALF).start()
            elif r != MARCH:
                out_copy(n, r).start()
            else:
                own_copy(n).start()
        if n < STEPS - 1:
            for r in range(ROWS):
                if r != MARCH:
                    out_copy(n, r).start()
            own_copy(n).start()
        if n == 0:
            shift(2).start()

    def share(n):
        for r in range(ROWS):
            stage[n, r] = row_sum(r).astype(BF16)
        twin_copy(n).start()

    def merged(n, r):
        return row_sum(r) + twin[n, r].astype(F32)

    def merge(n):
        twin_copy(n).wait_recv()

        @when(h == 5)
        def _():
            for r in ORDER:
                mixed[n, r] = merged(n, r).astype(BF16)
                tree_copy(n, r).start()

        for a, k, direct, via in ((3, 0, (4, 5, 6, 7), (0, 1, 2, 3)), (7, 1, (0, 1, 2, 3), (4, 5, 6, 7))):
            @when(h == a)
            def _(k=k, direct=direct, via=via):
                for r in direct:
                    mixed[n, r] = merged(n, r).astype(BF16)
                    far_copy(n, k, r).start()
                for r in via:
                    tree_copy(n, r).wait_recv()
                    mixed[n, r] = (merged(n, r) + tree[n, r % HALF].astype(F32)).astype(BF16)
                    far_copy(n, k, r).start()

    for i in range(3, len(loads)):
        load_wait(i)

    @when(h == MARCH)
    def _():
        for i in range(2):
            march_load(i).wait()

    halo_wait(0)
    halo_wait(1)

    @when(h != MARCH)
    def _():
        shift_wait(0)
        halo_start(2)

        @when(h < h_last)
        def _():
            shift(2).start()

    for n in range(STEPS):
        if n > 0:
            halo_wait(n + 1)
        products(n)

        @when(h == MARCH)
        def _(n=n):
            solve(n)

        @when(odd == 0)
        def _(n=n):
            share(n)

        @when((odd == 1) & (h != MARCH))
        def _(n=n):
            merge(n)

        @when(h != MARCH)
        def _(n=n):
            if n == 0:
                shift_wait(1)
                halo_start(3)
            if n == 1:
                @when(h > 1)
                def _():
                    shift(2).wait_recv()
                    halo_start(4)
            if n == 2:
                @when(h == 0)
                def _():
                    shift(2).wait_recv()
                    halo_start(4)

    @when(first)
    def _():
        for i in range(len(loads)):
            swap(i).wait_send()

    @when(odd == 0)
    def _():
        for n in range(STEPS):
            twin_copy(n).wait_send()

    @when((odd == 1) & (h != MARCH))
    def _():
        for n in range(STEPS):
            for r in range(ROWS):
                far_copy(n, 0, r).wait_send()

    for j in range(5):
        halo_sent(j)

    for j in range(3):
        @when((h < h_last) & ((h > 0) if j < 2 else (h >= 0)))
        def _(j=j):
            shift(j).wait_send()

    @when(h == MARCH)
    def _():
        for n in range(STEPS):
            own_copy(n).wait()
            for r in range(ROWS):
                if r != MARCH:
                    out_copy(n, r).wait_send()

    @when(h != MARCH)
    def _():
        for n in range(STEPS):
            out_copy(n, 0).wait_recv()


def on_device(zblocks, slot_row, slot_offset, slot_delay, history, inverse, excite):
    _, cap, bs, _ = zblocks.shape
    columns = history.shape[2]
    slots = zblocks[0]
    past = history.reshape(history.shape[0], ROWS, bs, columns)
    inv = inverse.reshape(ROWS, bs, bs)
    exc = excite.reshape(STEPS, ROWS, bs, columns)
    any_spec = pl.BlockSpec(memory_space=pl.ANY)
    block = (bs, columns)
    dma = pltpu.SemaphoreType.DMA
    return pl.pallas_call(
        kernel,
        out_shape=jax.ShapeDtypeStruct((STEPS, bs, columns), BF16),
        in_specs=[any_spec] * 7,
        out_specs=any_spec,
        scratch_shapes=[pltpu.VMEM((ROWS + 2 * R,) + block, BF16) for _ in range(6)]
        + [
            pltpu.VMEM((cap, bs, bs), BF16),
            pltpu.VMEM((cap + 1,) + block, F32),
            pltpu.VMEM((STEPS, ROWS) + block, BF16),
            pltpu.VMEM((STEPS, ROWS) + block, BF16),
            pltpu.VMEM((STEPS, ROWS) + block, BF16),
            pltpu.VMEM((STEPS, HALF) + block, BF16),
            pltpu.VMEM((STEPS, 2, ROWS) + block, BF16),
            pltpu.VMEM((STEPS, ROWS) + block, BF16),
            pltpu.VMEM((ROWS, bs, bs), BF16),
            pltpu.SMEM((1, cap), jnp.int32),
            pltpu.SMEM((1, cap), jnp.int32),
            pltpu.SMEM((1, cap), jnp.int32),
            pltpu.SMEM((cap,), jnp.int32),
            pltpu.SMEM((cap,), jnp.int32),
            pltpu.SMEM((ROWS,), jnp.int32),
            dma((8,)),
            dma((6,)),
            dma((5, 2)),
            dma((5, 2)),
            dma((3,)),
            dma((3,)),
            dma((STEPS,)),
            dma((STEPS,)),
            dma((STEPS, ROWS)),
            dma((STEPS, 2, ROWS)),
            dma((STEPS, HALF)),
            dma((STEPS, ROWS)),
            dma((STEPS,)),
        ],
        compiler_params=pltpu.CompilerParams(
            collective_id=0, has_side_effects=True, vmem_limit_bytes=60 * 1024 * 1024
        ),
    )(slots, slot_row, slot_offset, slot_delay, past, inv, exc)


def solution(mesh):
    return jax.shard_map(
        on_device,
        mesh=mesh,
        in_specs=(
            P("hist", "patch", None, None),
            P("hist", "patch"),
            P("hist", "patch"),
            P("hist", "patch"),
            P("hist", "patch", None),
            P("patch", None),
            P(None, "patch", None),
        ),
        out_specs=P(None, ("patch", "hist"), None),
        check_vma=False,
    )
```

time: 65.9 us -> 51 us (0.77)
  the two profiles are of different devices: /device:TPU:37 before, /device:TPU:35 now
where the time goes in v2:
time: 51 us; the launch traced here: 50.8 us
  Pallas kernels  49.3 us (97%)
  local copies, waits for them, and re-layouts  1.57 us (3%)
    pallas_call x1, Pallas kernels, on_device(): pl.pallas_call(kernel, out_shape=jax.ShapeDtypeStruct((STEPS, bs, columns...  49.3 us
    unnamed x1, local copies, waits for them, and re-layouts  1.57 us

profile of v2, /device:TPU:35, one launch (start us, length us, event | category | flops | bytes accessed | tf_op | source)
XLA Modules:
  0.0 50.8 jit_solution(5517474964763154988)
XLA Ops:
  0.0 49.3 %shard_map.73 = bf16[4,128,128]{2,1,0:T(8,128)(2,1)} custom-call(bf16[48,128,128]{2,1,0:T(8,128)(2,1)} %bitcast.4, s32[1,48]{1,0:T(1,128)} %row_hbm.1, s32[1,48]{1,0:T(1,128)} %off_hbm.1, s32[1,48]{1,0:T(1,128)} %dly_hbm.1, bf16[2,8,128,128]{3,2,1,0:T(8,128)(2,1)} %bitcast.6, bf16[8,128,128]{2,1,0:T(8,128)(2,1)} %bitcast.7, bf16[4,8,128,128]{3,2,1,0:T(8,128)(2,1)} %bitcast.5), custom_call_target="tpu_custom_call" | custom-call | tf_op jit(solution)/shard_map/pallas_call | solution.py:418
  49.3 1.6 %copy.9 = bf16[4,128,128]{2,1,0:T(8,128)(2,1)} copy(bf16[4,128,128]{2,1,0:T(8,128)(2,1)} %shard_map.73) | data formatting | bytes 262144

commit v3 on v2

v3 whole, which is shorter than its diff:
```python
import jax
import jax.numpy as jnp
from jax import lax
from jax.experimental import pallas as pl
from jax.experimental.pallas import tpu as pltpu
from jax.sharding import PartitionSpec as P

R = 4
STEPS = 4
ROWS = 8
HALF = ROWS // 2
GROUP = 8
MARCH = 1
BF16 = jnp.bfloat16
F32 = jnp.float32
ORDER = (0, 4, 1, 5, 2, 6, 3, 7)
LAST_ORDER = (4, 5, 6, 7, 2, 3, 0, 1)


def kernel(
    z_hbm, row_hbm, off_hbm, dly_hbm, hist_hbm, inv_hbm, exc_hbm, out_ref,
    xa, xb2, xb3, xb4, cur3, zbuf, sums, stage, twin, mixed, tree, far, excv, invv,
    row_s, off_s, dly_s, col_s, prev_s, last_s,
    go_sem, load_sem, swap_send, halo_send, halo_recv, shift_send, shift_recv,
    twin_send, twin_recv, red_send, far_first, far_recv, tree_first, tree_recv, out_send, own_send, out_recv,
):
    xb = (None, None, xb2, xb3, xb4)
    cap = z_hbm.shape[0]
    p = lax.axis_index("patch")
    h = lax.axis_index("hist")
    p_last = lax.axis_size("patch") - 1
    h_last = lax.axis_size("hist") - 1
    odd = h % 2
    first = h < 2
    later = h > 1
    lower = (h == MARCH) | (later & (odd == 0))
    upper = jnp.logical_not(lower)
    march = h == MARCH
    even = later & (odd == 0)
    gate = later & (odd == 1)
    has_left = p > 0
    has_right = p < p_last
    when = pl.when

    def at(patch=p, hist=h):
        return {"patch": patch, "hist": hist}

    barrier = pltpu.get_barrier_semaphore()

    def greet(where):
        pl.semaphore_signal(barrier, inc=1, device_id=where, device_id_type=pl.DeviceIdType.MESH)

    for side, q in ((has_left, p - 1), (has_right, p + 1)):
        @when(side & (h > 0))
        def _(q=q):
            greet(at(patch=q))

        @when(side & first)
        def _(q=q):
            greet(at(patch=q, hist=1 - h))

    lines = (
        (1, 2), (0, 2, 3, 4, 5, 6, 7), (0, 1, 3, 4), (1, 2, 4, 5),
        (1, 2, 3, 5, 6), (1, 3, 4, 6, 7), (1, 4, 5, 7), (1, 5, 6),
    )
    met = jnp.int32(0)
    for a, others in enumerate(lines):
        @when(h == a)
        def _(others=others):
            for b in others:
                greet(at(hist=b))

        met = jnp.where(h == a, len(others), met)
    sides = jnp.where(has_left, 1, 0) + jnp.where(has_right, 1, 0)
    met = met + sides * jnp.where(march, 2, 1)

    def remote(src, dst, ssem, rsem, where):
        return pltpu.make_async_remote_copy(
            src_ref=src, dst_ref=dst, send_sem=ssem, recv_sem=rsem,
            device_id=where, device_id_type=pl.DeviceIdType.MESH,
        )

    loads = (
        (row_hbm, row_s), (off_hbm, off_s), (dly_hbm, dly_s),
        (hist_hbm, xa.at[:, pl.ds(R, ROWS)]), (z_hbm, zbuf),
    )
    march_loads = ((inv_hbm, invv), (exc_hbm, excv))

    def load(i):
        return pltpu.make_async_copy(loads[i][0], loads[i][1], load_sem.at[i])

    def swap(i):
        return remote(loads[i][0], loads[i][1], swap_send.at[i], load_sem.at[i], at(hist=1 - h))

    def march_load(i):
        return pltpu.make_async_copy(march_loads[i][0], march_loads[i][1], load_sem.at[len(loads) + i])

    def load_wait(i):
        @when(first)
        def _():
            swap(i).wait_recv()

        @when(later)
        def _():
            load(i).wait()

    low, mid, high = pl.ds(0, R), pl.ds(R, ROWS), pl.ds(R + ROWS, R)

    partner = jnp.where(first, 1 - h, h)

    def own_left(i):
        return remote(
            hist_hbm.at[i, pl.ds(0, R)], xa.at[i, high], halo_send.at[0, i], halo_recv.at[0, 1], at(p - 1, partner)
        )

    def own_right(i):
        return remote(
            hist_hbm.at[i, pl.ds(ROWS - R, R)], xa.at[i, low], halo_send.at[1, i], halo_recv.at[0, 0], at(p + 1, partner)
        )

    def own_start():
        for i in (1, 0):
            @when(has_left)
            def _(i=i):
                own_left(i).start()

            @when(has_right)
            def _(i=i):
                own_right(i).start()

    def own_sent(i):
        @when(has_left)
        def _():
            own_left(i).wait_send()

        @when(has_right)
        def _():
            own_right(i).wait_send()

    def own_wait():
        @when(has_left)
        def _():
            remote(hist_hbm.at[:, pl.ds(0, R)], xa.at[:, low], halo_send.at[0, 0], halo_recv.at[0, 0], at(p - 1)).wait_recv()

        @when(has_right)
        def _():
            remote(hist_hbm.at[:, pl.ds(0, R)], xa.at[:, high], halo_send.at[0, 0], halo_recv.at[0, 1], at(p + 1)).wait_recv()

    def to_left(j, q=None):
        src, dst = (xb[j].at[pl.ds(R, R)], xb[j].at[high]) if q is None else (xb[j].at[R + q], xb[j].at[R + ROWS + q])
        return remote(src, dst, halo_send.at[0, j % 2], halo_recv.at[j - 1, 1], at(p - 1))

    def to_right(j, q=None):
        src, dst = (xb[j].at[pl.ds(ROWS, R)], xb[j].at[low]) if q is None else (xb[j].at[ROWS + q], xb[j].at[q])
        return remote(src, dst, halo_send.at[1, j % 2], halo_recv.at[j - 1, 0], at(p + 1))

    def halo_start(j):
        @when(has_left)
        def _():
            to_left(j).start()

        @when(has_right)
        def _():
            to_right(j).start()

    def halo_wait(j):
        @when(has_left)
        def _():
            to_right(j).wait_recv()

        @when(has_right)
        def _():
            to_left(j).wait_recv()

    def halo_sent(j):
        @when(has_left)
        def _():
            to_left(j).wait_send()

        @when(has_right)
        def _():
            to_right(j).wait_send()

    def cross(j):
        src, to = (hist_hbm.at[3 - j], h + 1) if j < 4 else (hist_hbm.at[1], h + 2)
        return remote(src, xb[j].at[mid], shift_send.at[j - 2], shift_recv.at[j - 2], at(hist=to))

    def inside(j):
        src = xa.at[3 - j] if j < 4 else xb2
        return remote(src, xb[j], shift_send.at[j - 2], shift_recv.at[j - 2], at(hist=h + 1 - 2 * odd))

    @when(later)
    def _():
        for i in range(len(loads)):
            load(i).start()

    @when(march)
    def _():
        for i in range(2):
            march_load(i).start()

    pl.semaphore_wait(barrier, met)

    @when(first | even)
    def _():
        own_start()

    @when((odd == 1) & (h < h_last))
    def _():
        cross(2).start()
        cross(3).start()

    @when(first)
    def _():
        for i in range(len(loads)):
            swap(i).start()

    @when(even)
    def _():
        own_sent(1)
        pl.semaphore_signal(go_sem, inc=1, device_id=at(hist=h + 1), device_id_type=pl.DeviceIdType.MESH)

    @when(gate)
    def _():
        pl.semaphore_wait(go_sem, 1)
        own_start()

    for edge, where in ((p == 0, low), (p == p_last, high)):
        @when(edge)
        def _(where=where):
            for i in range(2):
                xa[i, where] = jnp.zeros((R,) + xb2.shape[1:], BF16)

        @when(edge & lower)
        def _(where=where):
            for j in (2, 3, 4):
                xb[j][where] = jnp.zeros((R,) + xb2.shape[1:], BF16)

    sums[cap] = jnp.zeros(sums.shape[1:], F32)
    for i in range(3):
        load_wait(i)

    def note(s, last):
        row = row_s[0, s]
        col_s[s] = row + off_s[0, s]
        before = jnp.int32(cap)
        for r in range(ROWS):
            before = jnp.where(row == r, last[r], before)
        prev_s[s] = before
        return tuple(jnp.where(row == r, s, last[r]) for r in range(ROWS))

    last = lax.fori_loop(0, cap, note, (jnp.int32(cap),) * ROWS)
    for r in range(ROWS):
        last_s[r] = last[r]

    def products(n):
        for s in range(cap):
            col = col_s[s]
            delay = dly_s[0, s]
            if n == 0:
                x = xa[delay, col]
            else:
                x = jnp.where(delay == 1, xa[0, col] if n == 1 else xb[n][col], xb[n + 1][col])
            sums[s] = sums[prev_s[s]] + jnp.dot(zbuf[s], x, preferred_element_type=F32)

    def row_sum(r):
        return sums[last_s[r]]

    def twin_copy(n):
        return remote(stage.at[n], twin.at[n], twin_send, twin_recv.at[n], at(hist=h + 1))

    def far_copy(n, k, r):
        rsem = far_first.at[k, r % HALF] if n == 0 else far_recv.at[n - 1, k]
        return remote(mixed.at[n, r], far.at[n, k, r], red_send, rsem, at(hist=MARCH))

    def tree_copy(n, r):
        rsem = tree_first.at[r % HALF] if n == 0 else tree_recv.at[n - 1]
        return remote(mixed.at[n, r], tree.at[n, r % HALF], red_send, rsem, at(hist=3 if r < HALF else 7))

    def mixed_sent(n):
        remote(mixed.at[n], mixed.at[n], red_send, red_send, at(hist=MARCH)).wait_send()

    def far_wait(n, r):
        for k in range(2):
            if n == 0 and r < HALF:
                remote(mixed.at[0, pl.ds(0, 2)], far.at[0, k, pl.ds(0, 2)], red_send, far_first.at[k, r], at()).wait_recv()
            if n > 0 and r == 0:
                remote(mixed.at[n], far.at[n, k], red_send, far_recv.at[n - 1, k], at()).wait_recv()

    def tree_wait(n, r):
        if n == 0:
            tree_copy(n, r).wait_recv()
        elif r % HALF == 0:
            remote(mixed.at[n, pl.ds(0, HALF)], tree.at[n], red_send, tree_recv.at[n - 1], at()).wait_recv()

    def current_ref(n, r):
        return cur3.at[r] if n == STEPS - 1 else xb[n + 2].at[R + r]

    def out_copy(n, r):
        return remote(current_ref(n, r), out_ref.at[n], out_send, out_recv, at(hist=r))

    def own_copy(n):
        return pltpu.make_async_copy(current_ref(n, MARCH), out_ref.at[n], own_send)

    def out_start(n, r):
        if r == MARCH:
            own_copy(n).start()
        else:
            out_copy(n, r).start()

    def solve(n):
        twin_copy(n).wait_recv()
        if n == 0:
            own_sent(0)
            own_sent(1)
        if n == 2:
            halo_sent(2)
        if n > 0:
            far_wait(n, 0)
        for r in ORDER if n < STEPS - 1 else LAST_ORDER:
            if n == 0:
                far_wait(0, r)
            total = row_sum(r) + twin[n, r].astype(F32) + far[n, 0, r].astype(F32) + far[n, 1, r].astype(F32)
            residual = excv[n, r].astype(F32) - total
            coarse = residual.astype(BF16)
            fine = (residual - coarse.astype(F32)).astype(BF16)
            inverse = invv[r]
            current = jnp.dot(inverse, coarse, preferred_element_type=F32) + jnp.dot(
                inverse, fine, preferred_element_type=F32
            )
            current_ref(n, r)[...] = current.astype(BF16)
            if n == STEPS - 1:
                out_start(n, r)
            elif r < HALF:
                @when(has_left)
                def _(r=r):
                    to_left(n + 2, r).start()
            else:
                @when(has_right)
                def _(r=r):
                    to_right(n + 2, r - HALF).start()
        if n < STEPS - 1:
            for r in range(ROWS):
                out_start(n, r)

    def share(n):
        if n > 0:
            twin_copy(n - 1).wait_send()
        for r in range(ROWS):
            stage[n, r] = row_sum(r).astype(BF16)
        twin_copy(n).start()

    def merged(n, r):
        return row_sum(r) + twin[n, r].astype(F32)

    def merge(n):
        twin_copy(n).wait_recv()
        if n > 0:
            mixed_sent(n - 1)

        @when(h == 5)
        def _():
            for r in ORDER:
                mixed[n, r] = merged(n, r).astype(BF16)
                tree_copy(n, r).start()

        for a, k, direct, via in ((3, 0, (4, 5, 6, 7), (0, 1, 2, 3)), (7, 1, (0, 1, 2, 3), (4, 5, 6, 7))):
            @when(h == a)
            def _(k=k, direct=direct, via=via):
                for r in direct:
                    mixed[n, r] = merged(n, r).astype(BF16)
                    far_copy(n, k, r).start()
                for r in via:
                    tree_wait(n, r)
                    mixed[n, r] = (merged(n, r) + tree[n, r % HALF].astype(F32)).astype(BF16)
                    far_copy(n, k, r).start()

    for i in range(3, len(loads)):
        load_wait(i)

    @when(march)
    def _():
        for i in range(2):
            march_load(i).wait()

    own_wait()

    @when(march)
    def _():
        inside(2).start()
        inside(3).start()

    for n in range(STEPS):
        if n > 0:
            @when(lower)
            def _(n=n):
                halo_wait(n + 1)

            @when(upper)
            def _(n=n):
                inside(n + 1).wait_recv()

        products(n)

        @when(march)
        def _(n=n):
            solve(n)
            if n == 1:
                inside(4).start()

        @when(odd == 0)
        def _(n=n):
            share(n)

        @when(gate)
        def _(n=n):
            merge(n)

        if n == 0:
            @when(even)
            def _():
                inside(2).start()
                inside(3).start()
                cross(2).wait_recv()
                own_sent(0)
                halo_start(2)

            @when((odd == 0) & (h + 2 <= h_last))
            def _():
                cross(4).start()

            @when(even)
            def _():
                cross(3).wait_recv()
                halo_start(3)

        if n == 1:
            @when(even)
            def _():
                inside(4).start()
                cross(4).wait_recv()
                halo_sent(2)
                halo_start(4)

    @when(first)
    def _():
        for i in range(len(loads)):
            swap(i).wait_send()

    @when((h == 0) | gate)
    def _():
        own_sent(0)
        own_sent(1)

    @when(lower)
    def _():
        halo_sent(3)
        halo_sent(4)
        for j in (2, 3, 4):
            inside(j).wait_send()

    @when((odd == 1) & (h < h_last))
    def _():
        cross(2).wait_send()
        cross(3).wait_send()

    @when((odd == 0) & (h + 2 <= h_last))
    def _():
        cross(4).wait_send()

    @when(odd == 0)
    def _():
        twin_copy(STEPS - 1).wait_send()

    @when(gate)
    def _():
        mixed_sent(STEPS - 1)

    @when(march)
    def _():
        pltpu.make_async_copy(stage.at[0, pl.ds(0, STEPS)], out_ref, own_send).wait()
        remote(mixed.at[:, pl.ds(0, ROWS - 1)], mixed.at[:, pl.ds(0, ROWS - 1)], out_send, out_recv, at(hist=0)).wait_send()

    @when(jnp.logical_not(march))
    def _():
        remote(stage.at[0, pl.ds(0, STEPS)], out_ref, out_send, out_recv, at(hist=MARCH)).wait_recv()


def on_device(zblocks, slot_row, slot_offset, slot_delay, history, inverse, excite):
    _, cap, bs, _ = zblocks.shape
    columns = history.shape[2]
    slots = zblocks[0]
    past = history.reshape(history.shape[0], ROWS, bs, columns)
    inv = inverse.reshape(ROWS, bs, bs)
    exc = excite.reshape(STEPS, ROWS, bs, columns)
    operands = (slots, slot_row, slot_offset, slot_delay, past, inv, exc)
    any_spec = pl.BlockSpec(memory_space=pl.ANY)
    block = (bs, columns)
    dma = pltpu.SemaphoreType.DMA
    return pl.pallas_call(
        kernel,
        out_shape=pltpu.VMEM((STEPS, bs, columns), BF16),
        in_specs=[any_spec] * 7,
        out_specs=any_spec,
        scratch_shapes=[pltpu.VMEM((2, ROWS + 2 * R) + block, BF16)]
        + [pltpu.VMEM((ROWS + 2 * R,) + block, BF16) for _ in range(3)]
        + [
            pltpu.VMEM((ROWS,) + block, BF16),
            pltpu.VMEM((cap, bs, bs), BF16),
            pltpu.VMEM((cap + 1,) + block, F32),
            pltpu.VMEM((STEPS, ROWS) + block, BF16),
            pltpu.VMEM((STEPS, ROWS) + block, BF16),
            pltpu.VMEM((STEPS, ROWS) + block, BF16),
            pltpu.VMEM((STEPS, HALF) + block, BF16),
            pltpu.VMEM((STEPS, 2, ROWS) + block, BF16),
            pltpu.VMEM((STEPS, ROWS) + block, BF16),
            pltpu.VMEM((ROWS, bs, bs), BF16),
            pltpu.SMEM((1, cap), jnp.int32),
            pltpu.SMEM((1, cap), jnp.int32),
            pltpu.SMEM((1, cap), jnp.int32),
            pltpu.SMEM((cap,), jnp.int32),
            pltpu.SMEM((cap,), jnp.int32),
            pltpu.SMEM((ROWS,), jnp.int32),
            pltpu.SemaphoreType.REGULAR,
            dma((7,)),
            dma((5,)),
            dma((2, 2)),
            dma((4, 2)),
            dma((3,)),
            dma((3,)),
            dma,
            dma((STEPS,)),
            dma,
            dma((2, HALF)),
            dma((STEPS - 1, 2)),
            dma((HALF,)),
            dma((STEPS - 1,)),
            dma,
            dma,
            dma,
        ],
        compiler_params=pltpu.CompilerParams(
            collective_id=0, has_side_effects=True, vmem_limit_bytes=60 * 1024 * 1024
        ),
    )(*[pltpu.with_memory_space_constraint(v, pltpu.HBM) for v in operands])


def solution(mesh):
    return jax.shard_map(
        on_device,
        mesh=mesh,
        in_specs=(
            P("hist", "patch", None, None),
            P("hist", "patch"),
            P("hist", "patch"),
            P("hist", "patch"),
            P("hist", "patch", None),
            P("patch", None),
            P(None, "patch", None),
        ),
        out_specs=P(None, ("patch", "hist"), None),
        check_vma=False,
    )
```

time: 51 us -> 49.6 us (0.973)
  local copies, waits for them, and re-layouts: 1.57 us -> 0.66 us
    unnamed x1, local copies, waits for them, and re-layouts: 1.57 us -> 0.66 us
where the time goes in v3:
time: 49.6 us; the launch traced here: 49.5 us
  Pallas kernels  48.8 us (98%)
  local copies, waits for them, and re-layouts  0.66 us (1%)
    pallas_call x1, Pallas kernels, on_device(): pl.pallas_call(kernel, out_shape=pltpu.VMEM((STEPS, bs, columns), BF16),...  48.8 us

profile of v3, /device:TPU:35, one launch (start us, length us, event | category | flops | bytes accessed | tf_op | source)
XLA Modules:
  0.0 49.5 jit_solution(6122650417197198024)
XLA Ops:
  0.0 48.8 %shard_map.73 = bf16[4,128,128]{2,1,0:T(8,128)(2,1)S(1)} custom-call(bf16[48,128,128]{2,1,0:T(8,128)(2,1)} %bitcast.4, s32[1,48]{1,0:T(1,128)} %row_hbm.1, s32[1,48]{1,0:T(1,128)} %off_hbm.1, s32[1,48]{1,0:T(1,128)} %dly_hbm.1, bf16[2,8,128,128]{3,2,1,0:T(8,128)(2,1)} %bitcast.6, bf16[8,128,128]{2,1,0:T(8,128)(2,1)} %bitcast.7, bf16[4,8,128,128]{3,2,1,0:T(8,128)(2,1)} %bitcast.5), custom_call_target="tpu_custom_call" | custom-call | tf_op jit(solution)/shard_map/pallas_call | solution.py:500
  48.8 0.7 %copy.9 = bf16[4,128,128]{2,1,0:T(8,128)(2,1)} copy(bf16[4,128,128]{2,1,0:T(8,128)(2,1)S(1)} %shard_map.73) | data formatting | bytes 262144

commit v4 on v3

--- a/solution.py
+++ b/solution.py
@@ -11,16 +11,24 @@
 HALF = ROWS // 2
 GROUP = 8
 MARCH = 1
+FINE = 2
 BF16 = jnp.bfloat16
 F32 = jnp.float32
-ORDER = (0, 4, 1, 5, 2, 6, 3, 7)
+PARTS = ((0, 5), (1, 6), (2, 7), (3, 4))
+ORDER = tuple(r for part in PARTS for r in part)
 LAST_ORDER = (4, 5, 6, 7, 2, 3, 0, 1)
+LEFT = tuple((r, c) for r in range(HALF) for c in range(r, R))
+RIGHT = tuple((r, c) for r in range(HALF, ROWS) for c in range(R + ROWS, r + 2 * R + 1))
+PLACES = LEFT + RIGHT
+WIDTH = ROWS + 2 * R
+BY_ONE = (0, 1, 2, 3, 4)
+BY_THREE = (5, 6, 7)
 
 
 def kernel(
     z_hbm, row_hbm, off_hbm, dly_hbm, hist_hbm, inv_hbm, exc_hbm, out_ref,
-    xa, xb2, xb3, xb4, cur3, zbuf, sums, stage, twin, mixed, tree, far, excv, invv,
-    row_s, off_s, dly_s, col_s, prev_s, last_s,
+    xa, xb2, xb3, xb4, mid_only, cur3, dense, zbuf, sums, stage, twin, mixed, tree, far, base, excv, invv,
+    row_s, off_s, dly_s, col_s, prev_s, last_s, same_s, place_s,
     go_sem, load_sem, swap_send, halo_send, halo_recv, shift_send, shift_recv,
     twin_send, twin_recv, red_send, far_first, far_recv, tree_first, tree_recv, out_send, own_send, out_recv,
 ):
@@ -40,6 +48,7 @@
     gate = later & (odd == 1)
     has_left = p > 0
     has_right = p < p_last
+    far_right = p % 8 == 7
     when = pl.when
 
     def at(patch=p, hist=h):
@@ -108,34 +117,36 @@
 
     partner = jnp.where(first, 1 - h, h)
 
-    def own_left(i):
-        return remote(
-            hist_hbm.at[i, pl.ds(0, R)], xa.at[i, high], halo_send.at[0, i], halo_recv.at[0, 1], at(p - 1, partner)
-        )
-
-    def own_right(i):
-        return remote(
-            hist_hbm.at[i, pl.ds(ROWS - R, R)], xa.at[i, low], halo_send.at[1, i], halo_recv.at[0, 0], at(p + 1, partner)
-        )
+    pieces = ((1, R // 2, R // 2), (0, 0, R), (1, 0, R // 2))
+
+    def own_left(t):
+        i, first_block, blocks = pieces[t]
+        src = hist_hbm.at[i, pl.ds(first_block, blocks)]
+        dst = xa.at[i, pl.ds(R + ROWS + first_block, blocks)]
+        return remote(src, dst, halo_send.at[0, t // 2], halo_recv.at[0, 1], at(p - 1, partner))
+
+    def own_right(t):
+        i, first_block, blocks = pieces[t]
+        src = hist_hbm.at[i, pl.ds(ROWS - R + first_block, blocks)]
+        dst = xa.at[i, pl.ds(first_block, blocks)]
+        return remote(src, dst, halo_send.at[1, t // 2], halo_recv.at[0, 0], at(p + 1, partner))
 
     def own_start():
-        for i in (1, 0):
+        for t in (2, 0, 1):
             @when(has_left)
-            def _(i=i):
-                own_left(i).start()
+            def _(t=t):
+                own_left(t).start()
 
             @when(has_right)
-            def _(i=i):
-                own_right(i).start()
-
-    def own_sent(i):
-        @when(has_left)
-        def _():
-            own_left(i).wait_send()
-
-        @when(has_right)
-        def _():
-            own_right(i).wait_send()
+            def _(t=t):
+                own_right(t).start()
+
+    def own_sent(t):
+        some = xb2.at[pl.ds(0, R // 2 if t == 1 else R + R // 2)]
+        for side, present in enumerate((has_left, has_right)):
+            @when(present)
+            def _(side=side):
+                remote(some, some, halo_send.at[side, t], halo_recv.at[0, 0], at()).wait_send()
 
     def own_wait():
         @when(has_left)
@@ -253,14 +264,31 @@
     for r in range(ROWS):
         last_s[r] = last[r]
 
-    def products(n):
+    @when(march)
+    def _():
+        def note_place(s, seen):
+            place = jnp.where(dly_s[0, s] == 0, row_s[0, s] * WIDTH + col_s[s], -1)
+            before = jnp.int32(cap)
+            for k, (r, c) in enumerate(PLACES):
+                before = jnp.where(place == r * WIDTH + c, seen[k], before)
+            same_s[s] = before
+            return tuple(jnp.where(place == r * WIDTH + c, s, seen[k]) for k, (r, c) in enumerate(PLACES))
+
+        seen = lax.fori_loop(0, cap, note_place, (jnp.int32(cap),) * len(PLACES))
+        for k in range(len(PLACES)):
+            place_s[k] = seen[k]
+        mid_only[low] = jnp.zeros((R,) + xb2.shape[1:], BF16)
+        mid_only[high] = jnp.zeros((R,) + xb2.shape[1:], BF16)
+
+    def products(n, newest=None):
         for s in range(cap):
             col = col_s[s]
             delay = dly_s[0, s]
             if n == 0:
                 x = xa[delay, col]
             else:
-                x = jnp.where(delay == 1, xa[0, col] if n == 1 else xb[n][col], xb[n + 1][col])
+                new = xb[n + 1][col] if newest is None else newest[col]
+                x = jnp.where(delay == 1, xa[0, col] if n == 1 else xb[n][col], new)
             sums[s] = sums[prev_s[s]] + jnp.dot(zbuf[s], x, preferred_element_type=F32)
 
     def row_sum(r):
@@ -269,29 +297,35 @@
     def twin_copy(n):
         return remote(stage.at[n], twin.at[n], twin_send, twin_recv.at[n], at(hist=h + 1))
 
+    def part_of(r):
+        return [r in part for part in PARTS].index(True)
+
     def far_copy(n, k, r):
-        rsem = far_first.at[k, r % HALF] if n == 0 else far_recv.at[n - 1, k]
+        rsem = far_first.at[n, k, part_of(r)] if n < FINE else far_recv.at[n - FINE, k]
         return remote(mixed.at[n, r], far.at[n, k, r], red_send, rsem, at(hist=MARCH))
 
     def tree_copy(n, r):
-        rsem = tree_first.at[r % HALF] if n == 0 else tree_recv.at[n - 1]
-        return remote(mixed.at[n, r], tree.at[n, r % HALF], red_send, rsem, at(hist=3 if r < HALF else 7))
+        to, i = (3, r) if r in BY_ONE else (7, r - BY_THREE[0])
+        rsem = tree_first.at[n, i] if n < FINE else tree_recv.at[n - FINE]
+        return remote(mixed.at[n, r], tree.at[n, i], red_send, rsem, at(hist=to))
 
     def mixed_sent(n):
         remote(mixed.at[n], mixed.at[n], red_send, red_send, at(hist=MARCH)).wait_send()
 
-    def far_wait(n, r):
+    def far_wait(n, part):
         for k in range(2):
-            if n == 0 and r < HALF:
-                remote(mixed.at[0, pl.ds(0, 2)], far.at[0, k, pl.ds(0, 2)], red_send, far_first.at[k, r], at()).wait_recv()
-            if n > 0 and r == 0:
-                remote(mixed.at[n], far.at[n, k], red_send, far_recv.at[n - 1, k], at()).wait_recv()
-
-    def tree_wait(n, r):
-        if n == 0:
+            if n < FINE:
+                src, dst, rsem = mixed.at[n, pl.ds(0, 2)], far.at[n, k, pl.ds(0, 2)], far_first.at[n, k, part]
+            else:
+                src, dst, rsem = mixed.at[n], far.at[n, k], far_recv.at[n - FINE, k]
+            remote(src, dst, red_send, rsem, at()).wait_recv()
+
+    def tree_wait(n, rows, r):
+        if n < FINE:
             tree_copy(n, r).wait_recv()
-        elif r % HALF == 0:
-            remote(mixed.at[n, pl.ds(0, HALF)], tree.at[n], red_send, tree_recv.at[n - 1], at()).wait_recv()
+        elif r == rows[0]:
+            some = pl.ds(0, len(rows))
+            remote(mixed.at[n, some], tree.at[n, some], red_send, tree_recv.at[n - FINE], at()).wait_recv()
 
     def current_ref(n, r):
         return cur3.at[r] if n == STEPS - 1 else xb[n + 2].at[R + r]
@@ -308,37 +342,97 @@
         else:
             out_copy(n, r).start()
 
-    def solve(n):
+    def fold():
+        for slot in range(cap):
+            folded = jnp.dot(invv[row_s[0, slot]], zbuf[slot], preferred_element_type=F32)
+            zbuf[slot] = folded.astype(BF16)
+            sums[slot] = sums[same_s[slot]] + folded
+        for k in range(len(PLACES)):
+            dense[k] = sums[place_s[k]].astype(BF16)
+
+    def solved(n, r):
+        total = twin[n, r].astype(F32) + far[n, 0, r].astype(F32) + far[n, 1, r].astype(F32)
+        residual = excv[n, r].astype(F32) - total
+        coarse = residual.astype(BF16)
+        fine = (residual - coarse.astype(F32)).astype(BF16)
+        return jnp.dot(invv[r], coarse, preferred_element_type=F32) + jnp.dot(
+            invv[r], fine, preferred_element_type=F32
+        )
+
+    def keep(n, r, current):
+        current_ref(n, r)[...] = current
+        if n < STEPS - 1:
+            mid_only[R + r] = current
+
+    def send_row(n, r):
+        if n == STEPS - 1:
+            out_start(n, r)
+        elif r < HALF:
+            @when(has_left)
+            def _():
+                to_left(n + 2, r).start()
+        else:
+            @when(has_right)
+            def _():
+                to_right(n + 2, r - HALF).start()
+
+    def begin():
+        twin_copy(0).wait_recv()
+        own_sent(0)
+        own_sent(1)
+        for r in ORDER:
+            if r == PARTS[part_of(r)][0]:
+                far_wait(0, part_of(r))
+            keep(0, r, (solved(0, r) - row_sum(r)).astype(BF16))
+            send_row(0, r)
+        for r in range(ROWS):
+            out_start(0, r)
+
+    def advance(n):
+        products(n, mid_only)
         twin_copy(n).wait_recv()
-        if n == 0:
-            own_sent(0)
-            own_sent(1)
+        if n >= FINE:
+            far_wait(n, 0)
+        for r in ORDER:
+            if n < FINE and r == PARTS[part_of(r)][0]:
+                far_wait(n, part_of(r))
+            base[r] = solved(n, r) - row_sum(r)
         if n == 2:
             halo_sent(2)
-        if n > 0:
-            far_wait(n, 0)
-        for r in ORDER if n < STEPS - 1 else LAST_ORDER:
-            if n == 0:
-                far_wait(0, r)
-            total = row_sum(r) + twin[n, r].astype(F32) + far[n, 0, r].astype(F32) + far[n, 1, r].astype(F32)
-            residual = excv[n, r].astype(F32) - total
-            coarse = residual.astype(BF16)
-            fine = (residual - coarse.astype(F32)).astype(BF16)
-            inverse = invv[r]
-            current = jnp.dot(inverse, coarse, preferred_element_type=F32) + jnp.dot(
-                inverse, fine, preferred_element_type=F32
-            )
-            current_ref(n, r)[...] = current.astype(BF16)
-            if n == STEPS - 1:
-                out_start(n, r)
-            elif r < HALF:
-                @when(has_left)
-                def _(r=r):
-                    to_left(n + 2, r).start()
-            else:
-                @when(has_right)
-                def _(r=r):
-                    to_right(n + 2, r - HALF).start()
+
+        def left():
+            @when(has_left)
+            def _():
+                to_right(n + 1).wait_recv()
+
+            rows(range(HALF))
+
+        def right():
+            @when(has_right)
+            def _():
+                to_left(n + 1).wait_recv()
+
+            rows(range(HALF, ROWS))
+
+        def rows(some):
+            for r in some:
+                current = base[r]
+                for k, (row, c) in enumerate(PLACES):
+                    if row == r:
+                        current = current - jnp.dot(dense[k], xb[n + 1][c], preferred_element_type=F32)
+                keep(n, r, current.astype(BF16))
+                send_row(n, r)
+
+        @when(far_right)
+        def _():
+            left()
+            right()
+
+        @when(jnp.logical_not(far_right))
+        def _():
+            right()
+            left()
+
         if n < STEPS - 1:
             for r in range(ROWS):
                 out_start(n, r)
@@ -364,15 +458,15 @@
                 mixed[n, r] = merged(n, r).astype(BF16)
                 tree_copy(n, r).start()
 
-        for a, k, direct, via in ((3, 0, (4, 5, 6, 7), (0, 1, 2, 3)), (7, 1, (0, 1, 2, 3), (4, 5, 6, 7))):
+        for a, k, direct, via in ((3, 0, BY_THREE, BY_ONE), (7, 1, BY_ONE, BY_THREE)):
             @when(h == a)
             def _(k=k, direct=direct, via=via):
                 for r in direct:
                     mixed[n, r] = merged(n, r).astype(BF16)
                     far_copy(n, k, r).start()
                 for r in via:
-                    tree_wait(n, r)
-                    mixed[n, r] = (merged(n, r) + tree[n, r % HALF].astype(F32)).astype(BF16)
+                    tree_wait(n, via, r)
+                    mixed[n, r] = (merged(n, r) + tree[n, r - via[0]].astype(F32)).astype(BF16)
                     far_copy(n, k, r).start()
 
     for i in range(3, len(loads)):
@@ -382,6 +476,7 @@
     def _():
         for i in range(2):
             march_load(i).wait()
+        fold()
 
     own_wait()
 
@@ -391,8 +486,20 @@
         inside(3).start()
 
     for n in range(STEPS):
-        if n > 0:
-            @when(lower)
+        if n == 0:
+            @when(even)
+            def _():
+                cross(2).wait_recv()
+                own_sent(0)
+                halo_start(2)
+
+            products(0)
+
+            @when(march)
+            def _():
+                begin()
+        else:
+            @when(even)
             def _(n=n):
                 halo_wait(n + 1)
 
@@ -400,13 +507,15 @@
             def _(n=n):
                 inside(n + 1).wait_recv()
 
-        products(n)
-
-        @when(march)
-        def _(n=n):
-            solve(n)
-            if n == 1:
-                inside(4).start()
+            @when(march)
+            def _(n=n):
+                advance(n)
+                if n == 1:
+                    inside(4).start()
+
+            @when(jnp.logical_not(march))
+            def _(n=n):
+                products(n)
 
         @when(odd == 0)
         def _(n=n):
@@ -421,9 +530,6 @@
             def _():
                 inside(2).start()
                 inside(3).start()
-                cross(2).wait_recv()
-                own_sent(0)
-                halo_start(2)
 
             @when((odd == 0) & (h + 2 <= h_last))
             def _():
@@ -503,16 +609,18 @@
         in_specs=[any_spec] * 7,
         out_specs=any_spec,
         scratch_shapes=[pltpu.VMEM((2, ROWS + 2 * R) + block, BF16)]
-        + [pltpu.VMEM((ROWS + 2 * R,) + block, BF16) for _ in range(3)]
+        + [pltpu.VMEM((ROWS + 2 * R,) + block, BF16) for _ in range(4)]
         + [
             pltpu.VMEM((ROWS,) + block, BF16),
+            pltpu.VMEM((len(PLACES), bs, bs), BF16),
             pltpu.VMEM((cap, bs, bs), BF16),
             pltpu.VMEM((cap + 1,) + block, F32),
             pltpu.VMEM((STEPS, ROWS) + block, BF16),
             pltpu.VMEM((STEPS, ROWS) + block, BF16),
             pltpu.VMEM((STEPS, ROWS) + block, BF16),
-            pltpu.VMEM((STEPS, HALF) + block, BF16),
+            pltpu.VMEM((STEPS, len(BY_ONE)) + block, BF16),
             pltpu.VMEM((STEPS, 2, ROWS) + block, BF16),
+            pltpu.VMEM((ROWS,) + block, F32),
             pltpu.VMEM((STEPS, ROWS) + block, BF16),
             pltpu.VMEM((ROWS, bs, bs), BF16),
             pltpu.SMEM((1, cap), jnp.int32),
@@ -521,6 +629,8 @@
             pltpu.SMEM((cap,), jnp.int32),
             pltpu.SMEM((cap,), jnp.int32),
             pltpu.SMEM((ROWS,), jnp.int32),
+            pltpu.SMEM((cap,), jnp.int32),
+            pltpu.SMEM((len(PLACES),), jnp.int32),
             pltpu.SemaphoreType.REGULAR,
             dma((7,)),
             dma((5,)),
@@ -531,10 +641,10 @@
             dma,
             dma((STEPS,)),
             dma,
-            dma((2, HALF)),
-            dma((STEPS - 1, 2)),
-            dma((HALF,)),
-            dma((STEPS - 1,)),
+            dma((FINE, 2, HALF)),
+            dma((STEPS - FINE, 2)),
+            dma((FINE, len(BY_ONE))),
+            dma((STEPS - FINE,)),
             dma,
             dma,
             dma,

time: 49.6 us -> 47 us (0.948)
  Pallas kernels: 48.8 us -> 46.2 us
    pallas_call x1, Pallas kernels: 48.8 us -> 46.2 us  [on_device(): pl.pallas_call(kernel, out_shape=pltpu.VMEM((STEPS, bs, columns), BF16),...]
where the time goes in v4:
time: 47 us; the launch traced here: 46.9 us
  Pallas kernels  46.2 us (98%)
  local copies, waits for them, and re-layouts  0.66 us (1%)
    pallas_call x1, Pallas kernels, on_device(): pl.pallas_call(kernel, out_shape=pltpu.VMEM((STEPS, bs, columns), BF16),...  46.2 us

profile of v4, /device:TPU:35, one launch (start us, length us, event | category | flops | bytes accessed | tf_op | source)
XLA Modules:
  0.0 46.9 jit_solution(11343048636412864483)
XLA Ops:
  0.0 46.2 %shard_map.73 = bf16[4,128,128]{2,1,0:T(8,128)(2,1)S(1)} custom-call(bf16[48,128,128]{2,1,0:T(8,128)(2,1)} %bitcast.4, s32[1,48]{1,0:T(1,128)} %row_hbm.1, s32[1,48]{1,0:T(1,128)} %off_hbm.1, s32[1,48]{1,0:T(1,128)} %dly_hbm.1, bf16[2,8,128,128]{3,2,1,0:T(8,128)(2,1)} %bitcast.6, bf16[8,128,128]{2,1,0:T(8,128)(2,1)} %bitcast.7, bf16[4,8,128,128]{3,2,1,0:T(8,128)(2,1)} %bitcast.5), custom_call_target="tpu_custom_call" | custom-call | tf_op jit(solution)/shard_map/pallas_call | solution.py:606
  46.2 0.7 %copy.9 = bf16[4,128,128]{2,1,0:T(8,128)(2,1)} copy(bf16[4,128,128]{2,1,0:T(8,128)(2,1)S(1)} %shard_map.73) | data formatting | bytes 262144

commit v5 on v4

--- a/solution.py
+++ b/solution.py
@@ -14,22 +14,21 @@
 FINE = 2
 BF16 = jnp.bfloat16
 F32 = jnp.float32
-PARTS = ((0, 5), (1, 6), (2, 7), (3, 4))
+PARTS = ((3, 7), (2, 6), (1, 5), (0, 4))
 ORDER = tuple(r for part in PARTS for r in part)
-LAST_ORDER = (4, 5, 6, 7, 2, 3, 0, 1)
 LEFT = tuple((r, c) for r in range(HALF) for c in range(r, R))
 RIGHT = tuple((r, c) for r in range(HALF, ROWS) for c in range(R + ROWS, r + 2 * R + 1))
 PLACES = LEFT + RIGHT
 WIDTH = ROWS + 2 * R
-BY_ONE = (0, 1, 2, 3, 4)
-BY_THREE = (5, 6, 7)
+BY_ONE = (3, 2, 1, 0, 4)
+BY_THREE = (7, 6, 5)
 
 
 def kernel(
     z_hbm, row_hbm, off_hbm, dly_hbm, hist_hbm, inv_hbm, exc_hbm, out_ref,
     xa, xb2, xb3, xb4, mid_only, cur3, dense, zbuf, sums, stage, twin, mixed, tree, far, base, excv, invv,
     row_s, off_s, dly_s, col_s, prev_s, last_s, same_s, place_s,
-    go_sem, load_sem, swap_send, halo_send, halo_recv, shift_send, shift_recv,
+    go_sem, load_sem, swap_send, halo_send, halo_recv, block_recv, shift_send, shift_recv,
     twin_send, twin_recv, red_send, far_first, far_recv, tree_first, tree_recv, out_send, own_send, out_recv,
 ):
     xb = (None, None, xb2, xb3, xb4)
@@ -163,7 +162,8 @@
 
     def to_right(j, q=None):
         src, dst = (xb[j].at[pl.ds(ROWS, R)], xb[j].at[low]) if q is None else (xb[j].at[ROWS + q], xb[j].at[q])
-        return remote(src, dst, halo_send.at[1, j % 2], halo_recv.at[j - 1, 0], at(p + 1))
+        rsem = halo_recv.at[j - 1, 0] if q is None else block_recv.at[j - 2, q]
+        return remote(src, dst, halo_send.at[1, j % 2], rsem, at(p + 1))
 
     def halo_start(j):
         @when(has_left)
@@ -305,7 +305,7 @@
         return remote(mixed.at[n, r], far.at[n, k, r], red_send, rsem, at(hist=MARCH))
 
     def tree_copy(n, r):
-        to, i = (3, r) if r in BY_ONE else (7, r - BY_THREE[0])
+        to, i = (3, BY_ONE.index(r)) if r in BY_ONE else (7, BY_THREE.index(r))
         rsem = tree_first.at[n, i] if n < FINE else tree_recv.at[n - FINE]
         return remote(mixed.at[n, r], tree.at[n, i], red_send, rsem, at(hist=to))
 
@@ -400,28 +400,29 @@
         if n == 2:
             halo_sent(2)
 
+        def finish(r):
+            current = base[r]
+            for k, (row, c) in enumerate(PLACES):
+                if row == r:
+                    current = current - jnp.dot(dense[k], xb[n + 1][c], preferred_element_type=F32)
+            keep(n, r, current.astype(BF16))
+            send_row(n, r)
+
         def left():
-            @when(has_left)
-            def _():
-                to_right(n + 1).wait_recv()
-
-            rows(range(HALF))
+            for r in reversed(range(HALF)):
+                @when(has_left)
+                def _(r=r):
+                    to_right(n + 1, r).wait_recv()
+
+                finish(r)
 
         def right():
             @when(has_right)
             def _():
                 to_left(n + 1).wait_recv()
 
-            rows(range(HALF, ROWS))
-
-        def rows(some):
-            for r in some:
-                current = base[r]
-                for k, (row, c) in enumerate(PLACES):
-                    if row == r:
-                        current = current - jnp.dot(dense[k], xb[n + 1][c], preferred_element_type=F32)
-                keep(n, r, current.astype(BF16))
-                send_row(n, r)
+            for r in reversed(range(HALF, ROWS)):
+                finish(r)
 
         @when(far_right)
         def _():
@@ -466,7 +467,7 @@
                     far_copy(n, k, r).start()
                 for r in via:
                     tree_wait(n, via, r)
-                    mixed[n, r] = (merged(n, r) + tree[n, r - via[0]].astype(F32)).astype(BF16)
+                    mixed[n, r] = (merged(n, r) + tree[n, via.index(r)].astype(F32)).astype(BF16)
                     far_copy(n, k, r).start()
 
     for i in range(3, len(loads)):
@@ -538,6 +539,7 @@
             @when(even)
             def _():
                 cross(3).wait_recv()
+                halo_sent(2)
                 halo_start(3)
 
         if n == 1:
@@ -545,7 +547,6 @@
             def _():
                 inside(4).start()
                 cross(4).wait_recv()
-                halo_sent(2)
                 halo_start(4)
 
     @when(first)
@@ -636,6 +637,7 @@
             dma((5,)),
             dma((2, 2)),
             dma((4, 2)),
+            dma((STEPS - 1, R)),
             dma((3,)),
             dma((3,)),
             dma,

time: 47 us -> 45.7 us (0.972)
  the two profiles are of different devices: /device:TPU:35 before, /device:TPU:33 now
where the time goes in v5:
time: 45.7 us; the launch traced here: 45.6 us
  Pallas kernels  44.9 us (98%)
  local copies, waits for them, and re-layouts  0.66 us (1%)
    pallas_call x1, Pallas kernels, on_device(): pl.pallas_call(kernel, out_shape=pltpu.VMEM((STEPS, bs, columns), BF16),...  44.9 us

profile of v5, /device:TPU:33, one launch (start us, length us, event | category | flops | bytes accessed | tf_op | source)
XLA Modules:
  0.0 45.6 jit_solution(5862353639486343044)
XLA Ops:
  0.0 44.9 %shard_map.73 = bf16[4,128,128]{2,1,0:T(8,128)(2,1)S(1)} custom-call(bf16[48,128,128]{2,1,0:T(8,128)(2,1)} %bitcast.4, s32[1,48]{1,0:T(1,128)} %row_hbm.1, s32[1,48]{1,0:T(1,128)} %off_hbm.1, s32[1,48]{1,0:T(1,128)} %dly_hbm.1, bf16[2,8,128,128]{3,2,1,0:T(8,128)(2,1)} %bitcast.6, bf16[8,128,128]{2,1,0:T(8,128)(2,1)} %bitcast.7, bf16[4,8,128,128]{3,2,1,0:T(8,128)(2,1)} %bitcast.5), custom_call_target="tpu_custom_call" | custom-call | tf_op jit(solution)/shard_map/pallas_call | solution.py:607
  44.9 0.7 %copy.9 = bf16[4,128,128]{2,1,0:T(8,128)(2,1)} copy(bf16[4,128,128]{2,1,0:T(8,128)(2,1)S(1)} %shard_map.73) | data formatting | bytes 262144

commit v6 on v5

--- a/solution.py
+++ b/solution.py
@@ -28,7 +28,7 @@
     z_hbm, row_hbm, off_hbm, dly_hbm, hist_hbm, inv_hbm, exc_hbm, out_ref,
     xa, xb2, xb3, xb4, mid_only, cur3, dense, zbuf, sums, stage, twin, mixed, tree, far, base, excv, invv,
     row_s, off_s, dly_s, col_s, prev_s, last_s, same_s, place_s,
-    go_sem, load_sem, swap_send, halo_send, halo_recv, block_recv, shift_send, shift_recv,
+    go_sem, back_sem, load_sem, swap_send, halo_send, halo_recv, block_recv, shift_send, shift_recv,
     twin_send, twin_recv, red_send, far_first, far_recv, tree_first, tree_recv, out_send, own_send, out_recv,
 ):
     xb = (None, None, xb2, xb3, xb4)
@@ -219,7 +219,6 @@
     @when((odd == 1) & (h < h_last))
     def _():
         cross(2).start()
-        cross(3).start()
 
     @when(first)
     def _():
@@ -263,6 +262,17 @@
     last = lax.fori_loop(0, cap, note, (jnp.int32(cap),) * ROWS)
     for r in range(ROWS):
         last_s[r] = last[r]
+
+    @when((odd == 1) & (h < h_last))
+    def _():
+        cross(2).wait_send()
+        cross(3).start()
+
+    @when(gate)
+    def _():
+        own_sent(1)
+        own_sent(0)
+        pl.semaphore_signal(back_sem, inc=1, device_id=at(hist=h - 1), device_id_type=pl.DeviceIdType.MESH)
 
     @when(march)
     def _():
@@ -479,6 +489,13 @@
             march_load(i).wait()
         fold()
 
+    @when(even)
+    def _():
+        pl.semaphore_wait(back_sem, 1)
+        cross(2).wait_recv()
+        own_sent(0)
+        halo_start(2)
+
     own_wait()
 
     @when(march)
@@ -488,12 +505,6 @@
 
     for n in range(STEPS):
         if n == 0:
-            @when(even)
-            def _():
-                cross(2).wait_recv()
-                own_sent(0)
-                halo_start(2)
-
             products(0)
 
             @when(march)
@@ -554,7 +565,7 @@
         for i in range(len(loads)):
             swap(i).wait_send()
 
-    @when((h == 0) | gate)
+    @when(h == 0)
     def _():
         own_sent(0)
         own_sent(1)
@@ -568,7 +579,6 @@
 
     @when((odd == 1) & (h < h_last))
     def _():
-        cross(2).wait_send()
         cross(3).wait_send()
 
     @when((odd == 0) & (h + 2 <= h_last))
@@ -633,6 +643,7 @@
             pltpu.SMEM((cap,), jnp.int32),
             pltpu.SMEM((len(PLACES),), jnp.int32),
             pltpu.SemaphoreType.REGULAR,
+            pltpu.SemaphoreType.REGULAR,
             dma((7,)),
             dma((5,)),
             dma((2, 2)),

time: 45.7 us -> 44.4 us (0.972)
  the two profiles are of different devices: /device:TPU:33 before, /device:TPU:35 now
where the time goes in v6:
time: 44.4 us; the launch traced here: 43.9 us
  Pallas kernels  43.2 us (97%)
  local copies, waits for them, and re-layouts  0.66 us (1%)
    pallas_call x1, Pallas kernels, on_device(): pl.pallas_call(kernel, out_shape=pltpu.VMEM((STEPS, bs, columns), BF16),...  43.2 us

profile of v6, /device:TPU:35, one launch (start us, length us, event | category | flops | bytes accessed | tf_op | source)
XLA Modules:
  0.0 43.9 jit_solution(10081448038163292856)
XLA Ops:
  0.0 43.2 %shard_map.73 = bf16[4,128,128]{2,1,0:T(8,128)(2,1)S(1)} custom-call(bf16[48,128,128]{2,1,0:T(8,128)(2,1)} %bitcast.4, s32[1,48]{1,0:T(1,128)} %row_hbm.1, s32[1,48]{1,0:T(1,128)} %off_hbm.1, s32[1,48]{1,0:T(1,128)} %dly_hbm.1, bf16[2,8,128,128]{3,2,1,0:T(8,128)(2,1)} %bitcast.6, bf16[8,128,128]{2,1,0:T(8,128)(2,1)} %bitcast.7, bf16[4,8,128,128]{3,2,1,0:T(8,128)(2,1)} %bitcast.5), custom_call_target="tpu_custom_call" | custom-call | tf_op jit(solution)/shard_map/pallas_call | solution.py:617
  43.2 0.7 %copy.9 = bf16[4,128,128]{2,1,0:T(8,128)(2,1)} copy(bf16[4,128,128]{2,1,0:T(8,128)(2,1)S(1)} %shard_map.73) | data formatting | bytes 262144

commit v7 on v6

--- a/solution.py
+++ b/solution.py
@@ -58,7 +58,7 @@
     def greet(where):
         pl.semaphore_signal(barrier, inc=1, device_id=where, device_id_type=pl.DeviceIdType.MESH)
 
-    for side, q in ((has_left, p - 1), (has_right, p + 1)):
+    for side, q in ((has_right, p + 1), (has_left, p - 1)):
         @when(side & (h > 0))
         def _(q=q):
             greet(at(patch=q))
@@ -304,8 +304,15 @@
     def row_sum(r):
         return sums[last_s[r]]
 
-    def twin_copy(n):
-        return remote(stage.at[n], twin.at[n], twin_send, twin_recv.at[n], at(hist=h + 1))
+    def twin_copy(n, c):
+        some = pl.ds(HALF * c, HALF)
+        return remote(stage.at[n, some], twin.at[n, some], twin_send, twin_recv.at[n, c], at(hist=h + 1))
+
+    def twin_sent(n):
+        remote(stage.at[n], stage.at[n], twin_send, twin_send, at()).wait_send()
+
+    def twin_row(n, r):
+        return twin[n, ORDER.index(r)].astype(F32)
 
     def part_of(r):
         return [r in part for part in PARTS].index(True)
@@ -361,7 +368,7 @@
             dense[k] = sums[place_s[k]].astype(BF16)
 
     def solved(n, r):
-        total = twin[n, r].astype(F32) + far[n, 0, r].astype(F32) + far[n, 1, r].astype(F32)
+        total = twin_row(n, r) + far[n, 0, r].astype(F32) + far[n, 1, r].astype(F32)
         residual = excv[n, r].astype(F32) - total
         coarse = residual.astype(BF16)
         fine = (residual - coarse.astype(F32)).astype(BF16)
@@ -387,7 +394,8 @@
                 to_right(n + 2, r - HALF).start()
 
     def begin():
-        twin_copy(0).wait_recv()
+        twin_copy(0, 0).wait_recv()
+        twin_copy(0, 1).wait_recv()
         own_sent(0)
         own_sent(1)
         for r in ORDER:
@@ -400,7 +408,8 @@
 
     def advance(n):
         products(n, mid_only)
-        twin_copy(n).wait_recv()
+        twin_copy(n, 0).wait_recv()
+        twin_copy(n, 1).wait_recv()
         if n >= FINE:
             far_wait(n, 0)
         for r in ORDER:
@@ -450,29 +459,34 @@
 
     def share(n):
         if n > 0:
-            twin_copy(n - 1).wait_send()
-        for r in range(ROWS):
-            stage[n, r] = row_sum(r).astype(BF16)
-        twin_copy(n).start()
+            twin_sent(n - 1)
+        for i, r in enumerate(ORDER):
+            stage[n, i] = row_sum(r).astype(BF16)
+            if i % HALF == HALF - 1:
+                twin_copy(n, i // HALF).start()
 
     def merged(n, r):
-        return row_sum(r) + twin[n, r].astype(F32)
+        return row_sum(r) + twin_row(n, r)
 
     def merge(n):
-        twin_copy(n).wait_recv()
+        twin_copy(n, 0).wait_recv()
         if n > 0:
             mixed_sent(n - 1)
 
         @when(h == 5)
         def _():
-            for r in ORDER:
+            for i, r in enumerate(ORDER):
+                if i == HALF:
+                    twin_copy(n, 1).wait_recv()
                 mixed[n, r] = merged(n, r).astype(BF16)
                 tree_copy(n, r).start()
 
         for a, k, direct, via in ((3, 0, BY_THREE, BY_ONE), (7, 1, BY_ONE, BY_THREE)):
             @when(h == a)
             def _(k=k, direct=direct, via=via):
-                for r in direct:
+                for i, r in enumerate(direct):
+                    if i == 2:
+                        twin_copy(n, 1).wait_recv()
                     mixed[n, r] = merged(n, r).astype(BF16)
                     far_copy(n, k, r).start()
                 for r in via:
@@ -587,7 +601,7 @@
 
     @when(odd == 0)
     def _():
-        twin_copy(STEPS - 1).wait_send()
+        twin_sent(STEPS - 1)
 
     @when(gate)
     def _():
@@ -652,7 +666,7 @@
             dma((3,)),
             dma((3,)),
             dma,
-            dma((STEPS,)),
+            dma((STEPS, 2)),
             dma,
             dma((FINE, 2, HALF)),
             dma((STEPS - FINE, 2)),

time: 44.4 us -> 44.2 us (level)
  no operation moved by 1% of the time
where the time goes in v7:
time: 44.2 us; the launch traced here: 43.8 us
  Pallas kernels  43.1 us (98%)
  local copies, waits for them, and re-layouts  0.66 us (1%)
    pallas_call x1, Pallas kernels, on_device(): pl.pallas_call(kernel, out_shape=pltpu.VMEM((STEPS, bs, columns), BF16),...  43.1 us

profile of v7, /device:TPU:35, one launch (start us, length us, event | category | flops | bytes accessed | tf_op | source)
XLA Modules:
  0.0 43.8 jit_solution(10850460599666826698)
XLA Ops:
  0.0 43.1 %shard_map.73 = bf16[4,128,128]{2,1,0:T(8,128)(2,1)S(1)} custom-call(bf16[48,128,128]{2,1,0:T(8,128)(2,1)} %bitcast.4, s32[1,48]{1,0:T(1,128)} %row_hbm.1, s32[1,48]{1,0:T(1,128)} %off_hbm.1, s32[1,48]{1,0:T(1,128)} %dly_hbm.1, bf16[2,8,128,128]{3,2,1,0:T(8,128)(2,1)} %bitcast.6, bf16[8,128,128]{2,1,0:T(8,128)(2,1)} %bitcast.7, bf16[4,8,128,128]{3,2,1,0:T(8,128)(2,1)} %bitcast.5), custom_call_target="tpu_custom_call" | custom-call | tf_op jit(solution)/shard_map/pallas_call | solution.py:631
  43.1 0.7 %copy.9 = bf16[4,128,128]{2,1,0:T(8,128)(2,1)} copy(bf16[4,128,128]{2,1,0:T(8,128)(2,1)S(1)} %shard_map.73) | data formatting | bytes 262144
